TPU v7x, 32 devices: a whole 2x2x4 slice. The times are simulated.
32 devices in a mesh: dp: 16 (over z, x, core), head: 2 (over y).
Axes of the slice: x: 2, y: 2, z: 4, core: 2. Of those that a mesh axis runs over, the one named last changes fastest.
Arguments:
- layer_input: bfloat16 [16384, 1024], P('dp', 'head'), may hold values from -6 to 6
- ln_gain: bfloat16 [1024], P('head'), may hold values from 0.5 to 1.5
- up_x_weight: bfloat16 [1024, 2048], P(None, 'head'), may hold values from -0.1875 to 0.1875
- up_z_weight: bfloat16 [1024, 2048], P(None, 'head'), may hold values from -0.1875 to 0.1875
- conv_weight: bfloat16 [4, 2048], P(None, 'head'), may hold values from -3 to 3
- conv_bias: bfloat16 [2048], P('head'), may hold values from -3 to 3
- query_weight: bfloat16 [4, 2048], P(None, 'head'), may hold values from -3 to 3
- key_weight: bfloat16 [4, 2048], P(None, 'head'), may hold values from -3 to 3
- value_weight: bfloat16 [4, 2048], P(None, 'head'), may hold values from -3 to 3
- gate_weight: bfloat16 [3, 2048, 8], P(None, 'head'), may hold values from -0.078125 to 0.078125
- forget_bias: bfloat16 [4], replicated, may hold values from 3 to 6
- norm_gain: bfloat16 [2048], P('head'), may hold values from 0.5 to 1.5
- skip_gain: bfloat16 [2048], P('head'), may hold values from 0.25 to 1.75
- down_weight: bfloat16 [2048, 1024], P('head'), may hold values from -0.25 to 0.25
- cotangent: bfloat16 [16384, 1024], P('dp', 'head'), may hold values from -6 to 6
Outputs:
- layer_output: bfloat16 [16384, 1024], P('dp', 'head')
- input_grad: float32 [16384, 1024], P('dp', 'head')
- grad_ln_gain: float32 [1024], P('head')
- grad_up_x: float32 [1024, 2048], P(None, 'head')
- grad_up_z: float32 [1024, 2048], P(None, 'head')
- grad_conv_weight: float32 [4, 2048], P(None, 'head')
- grad_conv_bias: float32 [2048], P('head')
- grad_query_weight: float32 [4, 2048], P(None, 'head')
- grad_key_weight: float32 [4, 2048], P(None, 'head')
- grad_value_weight: float32 [4, 2048], P(None, 'head')
- grad_gate_weight: float32 [3, 2048, 8], P(None, 'head')
- grad_forget_bias: float32 [4], replicated
- grad_norm_gain: float32 [2048], P('head')
- grad_skip_gain: float32 [2048], P('head')
- grad_down: float32 [2048, 1024], P('head')
All inputs are finite; a program needn't handle non-finite values.
Results may differ from a plain program's by a relative error of at most 0.019.
The roundings to bfloat16 on the way count: a program that leaves them out, or rounds other values in their place, can miss the bound.
Values may be sent and summed in bfloat16 or wider, within the bound.
No kernel may reach another device: no remote copies, remote signals or barrier semaphores. Data moves between devices by JAX's collectives and lax.ppermute only.
A program may use at most 384 MiB of HBM per device.

v0:
```python
from functools import partial

import jax
import jax.numpy as jnp
from jax import lax
from jax.sharding import PartitionSpec as P

eps_norm = 1e-05
block_rows = 512
neg_big = -1e30


def matmul(first, second):
    return jnp.dot(
        first, second, precision=lax.Precision.HIGHEST, preferred_element_type=jnp.float32
    )


def layer_norm(rows, gain):
    center = jnp.mean(rows, axis=1, keepdims=True)
    spread = jnp.mean(rows * rows, axis=1, keepdims=True) - center * center
    return (rows - center) * lax.rsqrt(spread + eps_norm) * gain


def causal_conv(inputs, taps, bias_row):
    tap_count = taps.shape[0]
    length = inputs.shape[0]
    padded = jnp.pad(inputs, ((tap_count - 1, 0), (0, 0)))
    running = jnp.zeros_like(inputs) + bias_row
    for tap_index in range(tap_count):
        running = running + taps[tap_index] * padded[tap_index : tap_index + length]
    return running


def blockwise(inputs, taps):
    channels = inputs.shape[1]
    tap_count = taps.shape[0]
    phase_of = jnp.arange(channels) % tap_count
    running = jnp.zeros_like(inputs)
    for offset_shift in range(1 - tap_count, tap_count):
        coefficient = jnp.zeros((channels,), jnp.float32)
        for tap_index in range(tap_count):
            coefficient = coefficient + jnp.where(
                phase_of + offset_shift == tap_index, taps[tap_index], 0.0
            )
        running = running + coefficient * jnp.roll(inputs, -offset_shift, axis=1)
    return running


def head_block(carried_state, block_item):
    memory, normal, stabilizer = carried_state
    queries, key_rows, value_rows, inlet_gate, log_forget = block_item
    block_len, channels = queries.shape
    q_scale = channels ** (-0.5)
    cumulative = jnp.cumsum(log_forget)
    running = cumulative[-1]
    causal = jnp.arange(block_len)[:, None] >= jnp.arange(block_len)[None, :]
    decay_log = jnp.where(
        causal, cumulative[:, None] - cumulative[None, :] + inlet_gate[None, :], neg_big
    )
    carried = cumulative + stabilizer
    stable = jnp.maximum(carried, jnp.max(decay_log, axis=1))
    weights = jnp.exp(decay_log - stable[:, None])
    scores = matmul(queries, key_rows.T) * q_scale * weights
    carry_weight = jnp.exp(carried - stable)
    numerator = (
        matmul(scores, value_rows) + matmul(queries, memory) * q_scale * carry_weight[:, None]
    )
    denominator = jnp.sum(scores, axis=1) + matmul(queries, normal) * q_scale * carry_weight
    hidden = numerator / jnp.maximum(jnp.abs(denominator), jnp.exp(-stable))[:, None]
    fresh_log = running - cumulative + inlet_gate
    stab_next = jnp.maximum(running + stabilizer, jnp.max(fresh_log))
    keep_weight = jnp.exp(fresh_log - stab_next)
    weighted = key_rows * keep_weight[:, None]
    fade_factor = jnp.exp(running + stabilizer - stab_next)
    memory_next = memory * fade_factor + matmul(weighted.T, value_rows)
    normal_next = normal * fade_factor + jnp.sum(weighted, axis=0)
    return ((memory_next, normal_next, stab_next), hidden)


def one_head(queries, key_rows, value_rows, inlet_gate, forget_gate):
    length, channels = queries.shape
    block_len = min(block_rows, length)
    block_count = length // block_len
    log_forget = jax.nn.log_sigmoid(forget_gate)
    block_items = (
        queries.reshape(block_count, block_len, channels),
        key_rows.reshape(block_count, block_len, channels),
        value_rows.reshape(block_count, block_len, channels),
        inlet_gate.reshape(block_count, block_len),
        log_forget.reshape(block_count, block_len),
    )
    initial = (
        jnp.zeros((channels, channels), jnp.float32),
        jnp.zeros((channels,), jnp.float32),
        jnp.zeros((), jnp.float32),
    )
    last_state, hidden = lax.scan(jax.checkpoint(head_block), initial, block_items)
    return hidden.reshape(length, channels)


def mlstm_heads(queries, key_rows, value_rows, inlet_gate, forget_gate):
    length = queries.shape[0]
    head_count = inlet_gate.shape[1]
    channels = queries.shape[1] // head_count

    def to_heads(values):
        return values.reshape(length, head_count, channels).transpose(1, 0, 2)

    hidden = jax.vmap(one_head)(
        to_heads(queries), to_heads(key_rows), to_heads(value_rows), inlet_gate.T, forget_gate.T
    )
    return hidden.transpose(1, 0, 2).reshape(length, head_count * channels)


def group_norm(hidden, gain, head_count):
    length = hidden.shape[0]
    grouped = hidden.reshape(length, head_count, -1)
    center = grouped - jnp.mean(grouped, axis=2, keepdims=True)
    scaled = center * lax.rsqrt(jnp.mean(center * center, axis=2, keepdims=True) + eps_norm)
    return scaled.reshape(length, -1) * gain


def front(up_x, conv_taps, conv_offset, query_taps, key_taps, value_taps):
    conv_out = jax.nn.silu(causal_conv(up_x, conv_taps, conv_offset))
    return (
        blockwise(conv_out, query_taps),
        blockwise(conv_out, key_taps),
        blockwise(up_x, value_taps),
        conv_out,
    )


def tail(hidden, conv_out, up_z, gain_norm, gain_skip, head_count):
    return (group_norm(hidden, gain_norm, head_count) + gain_skip * conv_out) * jax.nn.silu(up_z)


def on_device(
    layer_input,
    ln_gain,
    up_x_weight,
    up_z_weight,
    conv_weight,
    conv_bias,
    query_weight,
    key_weight,
    value_weight,
    gate_weight,
    forget_bias,
    norm_gain,
    skip_gain,
    down_weight,
    cotangent,
):
    head_index = lax.axis_index("head")
    length, part_width = layer_input.shape
    all_heads = gate_weight.shape[2] // 2
    local_heads = all_heads // lax.axis_size("head")
    input_f = layer_input.astype(jnp.float32)
    rows_all, gain_all = (
        lax.all_gather(layer_input, "head", axis=1, tiled=True),
        lax.all_gather(ln_gain, "head", axis=0, tiled=True),
    )
    normed, norm_pull = jax.vjp(
        layer_norm, rows_all.astype(jnp.float32), gain_all.astype(jnp.float32)
    )
    normed_b = normed.astype(jnp.bfloat16)
    up_x = jnp.dot(normed_b, up_x_weight, preferred_element_type=jnp.float32)
    up_z = jnp.dot(normed_b, up_z_weight, preferred_element_type=jnp.float32)
    (queries, key_rows, value_rows, conv_out), front_pull = jax.vjp(
        front,
        up_x,
        conv_weight.astype(jnp.float32),
        conv_bias.astype(jnp.float32),
        query_weight.astype(jnp.float32),
        key_weight.astype(jnp.float32),
        value_weight.astype(jnp.float32),
    )
    queries_b = queries.astype(jnp.bfloat16)
    keys_b = key_rows.astype(jnp.bfloat16)
    values_b = value_rows.astype(jnp.bfloat16)
    gate_terms = (
        jnp.dot(queries_b, gate_weight[0], preferred_element_type=jnp.float32)
        + jnp.dot(keys_b, gate_weight[1], preferred_element_type=jnp.float32)
        + jnp.dot(values_b, gate_weight[2], preferred_element_type=jnp.float32)
    )
    gates = lax.psum(gate_terms.astype(jnp.bfloat16), "head").astype(jnp.float32)
    inlet_gate = lax.dynamic_slice_in_dim(gates, head_index * local_heads, local_heads, 1)
    forget_local = lax.dynamic_slice_in_dim(
        forget_bias.astype(jnp.float32), head_index * local_heads, local_heads, 0
    )
    forget_gate = (
        lax.dynamic_slice_in_dim(gates, all_heads + head_index * local_heads, local_heads, 1)
        + forget_local
    )
    queries_f = queries_b.astype(jnp.float32)
    keys_f = keys_b.astype(jnp.float32)
    values_f = values_b.astype(jnp.float32)
    hidden, cell_pull = jax.vjp(mlstm_heads, queries_f, keys_f, values_f, inlet_gate, forget_gate)
    gated_state, tail_pull = jax.vjp(
        partial(tail, head_count=local_heads),
        hidden,
        conv_out,
        up_z,
        norm_gain.astype(jnp.float32),
        skip_gain.astype(jnp.float32),
    )
    state_b = gated_state.astype(jnp.bfloat16)
    down_terms = jnp.dot(state_b, down_weight, preferred_element_type=jnp.float32)
    outcome = lax.psum_scatter(
        down_terms.astype(jnp.bfloat16), "head", scatter_dimension=1, tiled=True
    ).astype(jnp.float32)
    layer_output = (input_f + outcome).astype(jnp.bfloat16)
    grad_all = lax.all_gather(cotangent, "head", axis=1, tiled=True)
    grad_state = jnp.dot(grad_all, down_weight.T, preferred_element_type=jnp.float32)
    grad_down = jnp.dot(state_b.T, grad_all, preferred_element_type=jnp.float32)
    grad_hidden, grad_conv_out, grad_up_z, grad_norm_gain, grad_skip_gain = tail_pull(grad_state)
    grad_queries, grad_keys, grad_values, grad_inlet, grad_forget = cell_pull(grad_hidden)
    inlet_all, forget_all = (
        lax.all_gather(grad_inlet, "head", axis=1, tiled=True),
        lax.all_gather(grad_forget, "head", axis=1, tiled=True),
    )
    grad_gates = jnp.concatenate([inlet_all, forget_all], axis=1)
    gate_f = gate_weight.astype(jnp.float32)
    grad_queries = grad_queries + matmul(grad_gates, gate_f[0].T)
    grad_keys = grad_keys + matmul(grad_gates, gate_f[1].T)
    grad_values = grad_values + matmul(grad_gates, gate_f[2].T)
    grad_gate_weight = jnp.stack(
        [
            matmul(queries_f.T, grad_gates),
            matmul(keys_f.T, grad_gates),
            matmul(values_f.T, grad_gates),
        ]
    )
    grad_forget_bias = jnp.sum(forget_all, axis=0)
    (
        grad_up_x,
        grad_conv_weight,
        grad_conv_bias,
        grad_query_weight,
        grad_key_weight,
        grad_value_weight,
    ) = front_pull((grad_queries, grad_keys, grad_values, grad_conv_out))
    grad_upx_b = grad_up_x.astype(jnp.bfloat16)
    grad_upz_b = grad_up_z.astype(jnp.bfloat16)
    input_terms = jnp.dot(grad_upx_b, up_x_weight.T, preferred_element_type=jnp.float32) + jnp.dot(
        grad_upz_b, up_z_weight.T, preferred_element_type=jnp.float32
    )
    grad_upx_weight = jnp.dot(normed_b.T, grad_upx_b, preferred_element_type=jnp.float32)
    grad_upz_weight = jnp.dot(normed_b.T, grad_upz_b, preferred_element_type=jnp.float32)
    grad_normed = lax.psum(input_terms.astype(jnp.bfloat16), "head").astype(jnp.float32)
    grad_rows_all, grad_gain_all = norm_pull(grad_normed)
    grad_rows = lax.dynamic_slice_in_dim(grad_rows_all, head_index * part_width, part_width, 1)
    grad_ln_gain = lax.dynamic_slice_in_dim(grad_gain_all, head_index * part_width, part_width, 0)
    input_grad = cotangent.astype(jnp.float32) + grad_rows
    (
        grad_ln_gain,
        grad_upx_weight,
        grad_upz_weight,
        grad_conv_weight,
        grad_conv_bias,
        grad_query_weight,
        grad_key_weight,
        grad_value_weight,
        grad_gate_weight,
        grad_forget_bias,
        grad_norm_gain,
        grad_skip_gain,
        grad_down,
    ) = lax.psum(
        (
            grad_ln_gain,
            grad_upx_weight,
            grad_upz_weight,
            grad_conv_weight,
            grad_conv_bias,
            grad_query_weight,
            grad_key_weight,
            grad_value_weight,
            grad_gate_weight,
            grad_forget_bias,
            grad_norm_gain,
            grad_skip_gain,
            grad_down,
        ),
        "dp",
    )
    return (
        layer_output,
        input_grad,
        grad_ln_gain,
        grad_upx_weight,
        grad_upz_weight,
        grad_conv_weight,
        grad_conv_bias,
        grad_query_weight,
        grad_key_weight,
        grad_value_weight,
        grad_gate_weight,
        grad_forget_bias,
        grad_norm_gain,
        grad_skip_gain,
        grad_down,
    )


def solution(mesh):
    in_specs = (
        P("dp", "head"),
        P("head"),
        P(None, "head"),
        P(None, "head"),
        P(None, "head"),
        P("head"),
        P(None, "head"),
        P(None, "head"),
        P(None, "head"),
        P(None, "head", None),
        P(),
        P("head"),
        P("head"),
        P("head", None),
        P("dp", "head"),
    )
    out_specs = (
        P("dp", "head"),
        P("dp", "head"),
        P("head"),
        P(None, "head"),
        P(None, "head"),
        P(None, "head"),
        P("head"),
        P(None, "head"),
        P(None, "head"),
        P(None, "head"),
        P(None, "head", None),
        P(),
        P("head"),
        P("head"),
        P("head", None),
    )
    return jax.shard_map(
        on_device, mesh=mesh, in_specs=in_specs, out_specs=out_specs, check_vma=False
    )
```

profile of v0, /device:TPU:0, one launch (start us, length us, event | category | flops | bytes accessed | tf_op | source)
XLA Modules:
  0.0 1139.5 jit_solution(2209564164858787254)
XLA Ops:
  23.4 22.0 %all-gather.6.cloned.1.call-done = bf16[1024,1024]{1,0:T(8,128)(2,1)} async-done(((bf16[1024,512]{1,0:T(8,128)(2,1)}), bf16[1024,1024]{1,0:T(8,128)(2,1)}) %all-gather.6.cloned.1.call-update) | async-done | bytes 2097168 | tf_op jit(solution)/shard_map/all_gather | solution.py:161
  82.3 10.7 add_convert_fusion.1
  103.4 13.1 %add_convert_fusion.3 = bf16[1024,1024]{0,1:T(8,128)(2,1)} fusion(f32[1024]{0:T(1024)} %bitcast.11, f32[1024]{0:T(1024)} %bitcast.10, f32[1024]{0:T(1024)} %bitcast.9, f32[1024]{0:T(1024)S(1)} %bitcast.606, f32[1024]{0:T(1024)S(1)} %bitcast.610, f32[1024]{0:T(1024)S(1)} %bitcast.608, f32[1024]{0:T(1024)} %bitcast, f32[1024,1]{0,1:T(1,128)S(1)} %get-tuple-element.1005, ...), kind=kLoop, calls=%fused_computation.284 | loop fusion | flops 25165824 | bytes 31485952 | tf_op jit(solution)/shard_map/convert_element_type | solution.py:179
  118.6 8.3 add_convert_fusion.2
  130.8 7.0 psum.105
  154.0 56.4 %while.53 = (s32[]{:T(128)}, f32[2,512,512]{2,1,0:T(8,128)}, f32[2,512]{1,0:T(2,128)S(1)}, f32[2]{0:T(128)S(1)}, f32[2,2,512,512]{3,2,0,1:T(8,128)}, /*index=5*/...) while((s32[]{:T(128)}, f32[2,512,512]{2,1,0:T(8,128)}, ...), condition=%wide.region_10.11_spmd.clone, body=%wide.region_3.10_spmd.clone.sunk | while | flops 12906021888 | bytes 156184784 | solution.py:98
  203.2 7.0 multiply_add_fusion.10
  218.6 10.2 broadcast_multiply_fusion.2
  253.6 230.7 %while.54 = (s32[]{:T(128)}, f32[2,512,512]{2,1,0:T(8,128)}, f32[2,512]{1,0:T(2,128)S(1)}, f32[2]{0:T(128)S(1)}, f32[2,2,512,512]{3,2,0,1:T(8,128)}, /*index=5*/...) while((s32[]{:T(128)}, f32[2,512,512]{2,1,0:T(8,128)}, ...), condition=%wide.region_37.38_spmd.clone, body=%wide.region_16.37_spmd.clone.sunk | while | flops 35494371328 | bytes 369942208 | solution.py:98
  276.9 7.1 convert_reduce_fusion.5
  342.9 8.0 bitcast_dynamic-update-slice_fusion.15
  353.1 11.2 multiply_add_fusion.11
  388.3 7.1 convert_reduce_fusion.5
  454.4 8.0 bitcast_dynamic-update-slice_fusion.15
  464.5 11.2 multiply_add_fusion.11
  516.6 27.7 %multiply_reduce_fusion.15 = (f32[1024]{0:T(1024)}, f32[1024]{0:T(1024)}, f32[1024]{0:T(1024)}, f32[1024]{0:T(1024)}, f32[1024]{0:T(1024)}, /*index=5*/f32[1024]...) fusion(f32[1024,1023]{0,1:T(8,128)} %get-tuple-element.1006, ...), kind=kOutput, calls=%fused_computation.260 | convolution fusion | flops 148897792 | bytes 71417856 | tf_op jit(solution)/shard_map/dot_general | solution.py:14
  544.4 13.5 %multiply_reduce_fusion.14 = (f32[1024]{0:T(1024)}, f32[1024]{0:T(1024)S(1)}, f32[1024]{0:T(1024)}, f32[1024]{0:T(1024)}, f32[1024]{0:T(1024)S(1)}, /*index=5*/f...) fusion(f32[1024,1024]{0,1:T(8,128)} %get-tuple-element.1125, ...), kind=kLoop, calls=%fused_computation.259 | loop fusion | flops 27254784 | bytes 50388992 | tf_op jit(solution)/shard_map/transpose(jvp())/reduce_sum | solution.py:46
  588.0 45.3 %multiply_reduce_fusion.12 = (f32[1024]{0:T(1024)S(1)}, f32[1024]{0:T(1024)}, f32[1024]{0:T(1024)}, f32[1024]{0:T(1024)}, f32[1024]{0:T(1024)}, /*index=5*/f32[1...) fusion(f32[1024,3]{0,1:T(4,128)S(1)} %copy-done.79, ...), kind=kOutput, calls=%fused_computation.257 | convolution fusion | flops 171962368 | bytes 109187072 | tf_op jit(solution)/shard_map/dot_general | solution.py:14
  633.3 11.5 %broadcast_multiply_fusion.3 = (f32[1024,1024]{0,1:T(8,128)S(1)}, f32[1024,1024]{0,1:T(8,128)S(1)}, f32[1024,1024]{0,1:T(8,128)S(1)}, f32[1024,1024]{0,1:T(8,128...) fusion(f32[1024,1024]{0,1:T(8,128)} %get-tuple-element.1126, ...), kind=kLoop, calls=%fused_computation.299 | loop fusion | flops 10485760 | bytes 50372608 | tf_op jit(solution)/shard_map/transpose(jvp())/mul | solution.py:46
  656.6 14.9 %fusion.130 = bf16[1024,1024]{0,1:T(8,128)(2,1)S(1)} fusion(f32[1024,1024]{0,1:T(8,128)} %get-tuple-element.1129, f32[1024,1024]{0,1:T(8,128)} %get-tuple-element.1128, f32[1024,1024]{0,1:T(8,128)} %get-tuple-element.1127, f32[1024,1024]{0,1:T(8,128)} %get-tuple-element.1130, f32[1024,3]{0,1:T(4,128)S(1)} %copy-done.75, f32[1024,1021]{0,1:T(8,128)} %split.166, ...), kind=kLoop, calls=%fused_computation.226 | loop fusion | flops 18874368 | bytes 48238592 | tf_op jit(solution)/shard_map/convert_element_type | solution.py:244
  712.6 31.9 %all-reduce.136.cloned.1.call-done = bf16[1024,1024]{1,0:T(8,128)(2,1)} async-done(((bf16[1024,1024]{1,0:T(8,128)(2,1)}), bf16[1024,1024]{1,0:T(8,128)(2,1)}) %all-reduce.136.cloned.1.call-update) | async-done | bytes 2097168 | tf_op jit(solution)/shard_map/psum | solution.py:251
  756.8 21.7 %reduce-scatter.2.cloned.1.call-done = bf16[1024,512]{1,0:T(8,128)(2,1)} async-done(((bf16[1024,1024]{1,0:T(8,128)(2,1)}), bf16[1024,512]{1,0:T(8,128)(2,1)}) %reduce-scatter.2.cloned.1.call-update) | async-done | bytes 1048592 | tf_op jit(solution)/shard_map/reduce_scatter | solution.py:210
  781.0 90.7 %all-reduce.138.cloned.1.call-done = (f32[512]{0:T(512)}, f32[4,1024]{1,0:T(4,128)}, f32[1024]{0:T(1024)}, f32[4,1024]{1,0:T(4,128)}, f32[4,1024]{1,0:T(4,128)},...) async-done(((f32[512]{0:T(512)}, f32[4,1024]{1,0:T(4,128)}, f32[1024]{0:T(1024)}, f32[4,1024]{1,0:T(4,128)}, f32[4,1024]{1,0:T(4,128)}, ...) | async-done | bytes 79904 | tf_op jit(solution)/shard_map/psum | solution.py:270
  871.7 244.9 %all-reduce.140.cloned.1.call-done = (f32[1024,1024]{1,0:T(8,128)}, f32[1024,1024]{1,0:T(8,128)}, f32[3,1024,8]{1,2,0:T(8,128)}, f32[1024,1024]{1,0:T(8,128)}) async-done(((f32[1024,1024]{1,0:T(8,128)}, f32[1024,1024]{1,0:T(8,128)}, f32[3,1024,8]{1,2,0:T(8,128)}, f32[1024,1024]{1,0:T(8,128)}), (f32[1024,1024]{1,0:T(8,128)}, f32[1024,1024]{1,0:T(8,128)}, f32[3,1024,8]{1,2,0:T(8,128)}, ...) | async-done | bytes 12681232 | tf_op jit(solution)/shard_map/psum | solution.py:270
  (770 shorter events, 479.6 us)
Async XLA Ops:
  7.2 211.4 %copy-start = (bf16[1024,1024]{1,0:T(8,128)(2,1)S(1)}, bf16[1024,1024]{1,0:T(8,128)(2,1)}, u32[]{:S(2)}) copy-start(bf16[1024,1024]{1,0:T(8,128)(2,1)} %param.32) | copy-start | bytes 6291460
  7.2 38.2 %all-gather.6.cloned.1.call-start = ((), (), s32[]{:S(2)}) async-start(), calls=%async_computation.1 | async-start | bytes 3145728 | tf_op jit(solution)/shard_map/all_gather | solution.py:161
  7.9 210.6 %all-gather.8.cloned.1.call-start = ((), (), s32[]{:S(2)}) async-start(), calls=%async_computation.3 | async-start | bytes 3145728 | tf_op jit(solution)/shard_map/all_gather | solution.py:214
  8.7 735.8 %all-reduce.136.cloned.1.call-start = ((), (), s32[]{:S(2)}) async-start(), calls=%async_computation.4 | async-start | bytes 4194304 | tf_op jit(solution)/shard_map/psum | solution.py:251
  9.5 72.7 %copy-start.102 = (f32[1,1024]{1,0:T(1,128)}, f32[1,1024]{1,0:T(1,128)S(1)}, u32[]{:S(2)}) copy-start(f32[1,1024]{1,0:T(1,128)S(1)} %get-tuple-element.1009) | copy-start | bytes 12292
  9.5 72.7 %copy-start.104 = (f32[1,1024]{1,0:T(1,128)}, f32[1,1024]{1,0:T(1,128)S(1)}, u32[]{:S(2)}) copy-start(f32[1,1024]{1,0:T(1,128)S(1)} %get-tuple-element.1010) | copy-start | bytes 12292
  9.5 72.7 %copy-start.106 = (f32[1,1024]{1,0:T(1,128)}, f32[1,1024]{1,0:T(1,128)S(1)}, u32[]{:S(2)}) copy-start(f32[1,1024]{1,0:T(1,128)S(1)} %get-tuple-element.1011) | copy-start | bytes 12292
  9.5 72.7 %copy-start.108 = (f32[1,1024]{1,0:T(1,128)}, f32[1,1024]{1,0:T(1,128)S(1)}, u32[]{:S(2)}) copy-start(f32[1,1024]{1,0:T(1,128)S(1)} %get-tuple-element.1012) | copy-start | bytes 12292
  10.3 108.1 %copy-start.110 = (f32[1,1024]{1,0:T(1,128)}, f32[1,1024]{1,0:T(1,128)S(1)}, u32[]{:S(2)}) copy-start(f32[1,1024]{1,0:T(1,128)S(1)} %get-tuple-element.1016) | copy-start | bytes 12292
  10.3 108.1 %copy-start.112 = (f32[1,1024]{1,0:T(1,128)}, f32[1,1024]{1,0:T(1,128)S(1)}, u32[]{:S(2)}) copy-start(f32[1,1024]{1,0:T(1,128)S(1)} %get-tuple-element.1017) | copy-start | bytes 12292
  10.3 108.1 %copy-start.114 = (f32[1,1024]{1,0:T(1,128)}, f32[1,1024]{1,0:T(1,128)S(1)}, u32[]{:S(2)}) copy-start(f32[1,1024]{1,0:T(1,128)S(1)} %get-tuple-element.1018) | copy-start | bytes 12292
  10.4 108.1 %copy-start.116 = (f32[1,1024]{1,0:T(1,128)}, f32[1,1024]{1,0:T(1,128)S(1)}, u32[]{:S(2)}) copy-start(f32[1,1024]{1,0:T(1,128)S(1)} %get-tuple-element.1019) | copy-start | bytes 12292
  10.4 108.0 %copy-start.98 = (f32[1,1024]{1,0:T(1,128)}, f32[1,1024]{1,0:T(1,128)S(1)}, u32[]{:S(2)}) copy-start(f32[1,1024]{1,0:T(1,128)S(1)} %get-tuple-element.1020) | copy-start | bytes 12292
  10.4 108.0 %copy-start.100 = (f32[1,1024]{1,0:T(1,128)}, f32[1,1024]{1,0:T(1,128)S(1)}, u32[]{:S(2)}) copy-start(f32[1,1024]{1,0:T(1,128)S(1)} %get-tuple-element.1021) | copy-start | bytes 12292
  10.4 108.0 %copy-start.146 = (f32[1,1024]{1,0:T(1,128)}, f32[1,1024]{1,0:T(1,128)S(1)}, u32[]{:S(2)}) copy-start(f32[1,1024]{1,0:T(1,128)S(1)} %get-tuple-element.1022) | copy-start | bytes 12292
  11.8 90.2 %copy-start.148 = (f32[1,1024]{1,0:T(1,128)}, f32[1,1024]{1,0:T(1,128)S(1)}, u32[]{:S(2)}) copy-start(f32[1,1024]{1,0:T(1,128)S(1)} %get-tuple-element.1029) | copy-start | bytes 12292
  11.8 90.2 %copy-start.150 = (f32[1,1024]{1,0:T(1,128)}, f32[1,1024]{1,0:T(1,128)S(1)}, u32[]{:S(2)}) copy-start(f32[1,1024]{1,0:T(1,128)S(1)} %get-tuple-element.1027) | copy-start | bytes 12292
  11.8 90.2 %copy-start.152 = (f32[1,1024]{1,0:T(1,128)}, f32[1,1024]{1,0:T(1,128)S(1)}, u32[]{:S(2)}) copy-start(f32[1,1024]{1,0:T(1,128)S(1)} %get-tuple-element.1028) | copy-start | bytes 12292
  18.0 195.2 %copy-start.126 = (f32[2,1,512]{2,1,0:T(1,128)}, f32[2,1,512]{2,1,0:T(1,128)S(1)}, u32[]{:S(2)}) copy-start(f32[2,1,512]{2,1,0:T(1,128)S(1)} %convert_element_type.128) | copy-start | bytes 12292
  47.7 165.4 %copy-start.128 = (f32[1024]{0:T(1024)}, f32[1024]{0:T(1024)S(1)}, u32[]{:S(2)}) copy-start(f32[1024]{0:T(1024)S(1)} %get-tuple-element.1122) | copy-start | bytes 12292
  47.7 165.4 %copy-start.130 = (f32[1024]{0:T(1024)}, f32[1024]{0:T(1024)S(1)}, u32[]{:S(2)}) copy-start(f32[1024]{0:T(1024)S(1)} %get-tuple-element.1123) | copy-start | bytes 12292
  680.2 98.3 %reduce-scatter.2.cloned.1.call-start = ((), (), s32[]{:S(2)}) async-start(), calls=%async_computation.2 | async-start | bytes 3145728 | tf_op jit(solution)/shard_map/reduce_scatter | solution.py:210
  686.8 184.9 %all-reduce.138.cloned.1.call-start = ((), (), s32[]{:S(2)}) async-start(), calls=%async_computation.5 | async-start | bytes 160768 | tf_op jit(solution)/shard_map/psum | solution.py:270
  750.5 366.2 %all-reduce.140.cloned.1.call-start = ((), (), s32[]{:S(2)}) async-start(), calls=%async_computation.6 | async-start | bytes 25362432 | tf_op jit(solution)/shard_map/psum | solution.py:270
  (202 other events, 2600.6 us)
Sparse Core Ops, SparseCore 0:
  9.6 35.8 all-gather.5
  47.0 33.1 all-gather.7
  680.4 64.0 all-reduce.135
  746.7 31.8 reduce-scatter.1
  784.1 87.6 all-reduce.137
  878.0 238.5 all-reduce.139
where the time goes:
time: 1150 us; the launch traced here: 1140 us
  waiting for transfers between devices  413 us (36%)
  matrix products  333 us (29%)
  local copies, waits for them, and re-layouts  199 us (17%)
  other arithmetic  146 us (13%)
  blocking collectives  20.9 us (2%)
  between operations  16.6 us (1%)
    psum x2, waiting for transfers between devices, on_device(): lax.psum((grad_ln_gain, grad_upx_weight, grad_upz_weight, grad_conv_weigh...  336 us
    dot_general x42, matrix products, matmul(): jnp.dot(first, second, precision=lax.Precision.HIGHEST, preferred_element...  280 us
    unnamed x342, local copies, waits for them, and re-layouts  38.1 us
    psum x1, waiting for transfers between devices, on_device(): lax.psum(input_terms.astype(jnp.bfloat16), 'head').astype(jnp.float32)  31.9 us
    split x27, local copies, waits for them, and re-layouts, blockwise(): running = running + coefficient * jnp.roll(inputs, -offset_shift, axis=1)  28.4 us
  transfers between devices with their start and end apart: 6, of which 5 were waited for; matrix products, arithmetic and copies ran while one was open for 19% of the time, Pallas kernels for 0%

commit v1 on v0

v1 whole, which is shorter than its diff:
```python
from functools import partial

import jax
import jax.numpy as jnp
from jax import lax
from jax.experimental import pallas as pl
from jax.experimental.pallas import tpu as pltpu
from jax.sharding import PartitionSpec as P

eps_norm = 1e-05
group = 256
block = 256
b16 = jnp.bfloat16
f32 = jnp.float32


def dot_nn(first, second):
    return lax.dot_general(first, second, (((1,), (0,)), ((), ())), preferred_element_type=f32)


def dot_nt(first, second):
    return lax.dot_general(first, second, (((1,), (1,)), ((), ())), preferred_element_type=f32)


def dot_tn(first, second):
    return lax.dot_general(first, second, (((0,), (0,)), ((), ())), preferred_element_type=f32)


def sigmoid(values):
    return 0.5 * jnp.tanh(0.5 * values) + 0.5


def spec(shape, index_map):
    return pl.BlockSpec(shape, index_map)


def whole(shape):
    return pl.BlockSpec(shape, lambda *_: (0,) * len(shape))


def smem():
    return pl.BlockSpec(memory_space=pltpu.SMEM)


def shape_of(shape, dtype):
    return jax.ShapeDtypeStruct(shape, dtype)


def settings(mebibytes):
    return pltpu.CompilerParams(
        dimension_semantics=("arbitrary",), vmem_limit_bytes=mebibytes * 2**20
    )


def cost(micros):
    return pl.CostEstimate(
        flops=int(micros * 1.1e9), bytes_accessed=int(micros * 3.6e6), transcendentals=0
    )


def side_cols(side, width):
    return pl.ds(pl.multiple_of(side * width, width), width)


def spread_taps(taps):
    tap_count, width = taps.shape
    rows = lax.broadcasted_iota(jnp.int32, (width, width), 0) // tap_count
    cols = lax.broadcasted_iota(jnp.int32, (width, width), 1) // tap_count
    pair = jnp.concatenate([taps.astype(f32)] * (8 // tap_count), axis=0)
    full = jnp.concatenate([pair] * (width // 8), axis=0)
    return jnp.where(rows == cols, full, 0.0).astype(b16)


def gather_taps(dense, tap_count):
    width = dense.shape[0]
    rows = lax.broadcasted_iota(jnp.int32, (width, width), 0) // tap_count
    cols = lax.broadcasted_iota(jnp.int32, (width, width), 1) // tap_count
    kept = jnp.where(rows == cols, dense, 0.0)
    folded = jnp.sum(kept.reshape(width // 8, 8, width), axis=0)
    total = folded[:tap_count]
    for part in range(1, 8 // tap_count):
        total = total + folded[part * tap_count : (part + 1) * tap_count]
    return total


def row_stats(own, other):
    width = own.shape[1] + other.shape[1]
    total = jnp.sum(own, axis=1, keepdims=True) + jnp.sum(other, axis=1, keepdims=True)
    square = jnp.sum(own * own, axis=1, keepdims=True) + jnp.sum(
        other * other, axis=1, keepdims=True
    )
    center = total / width
    return center, lax.rsqrt(square / width - center * center + eps_norm)


def seat_rows(values, seats_ref, out_ref):
    seats = seats_ref.shape[0]
    height = values.shape[0] // seats
    for piece in range(seats):
        out_ref[pl.ds(pl.multiple_of(seats_ref[piece] * height, height), height), :] = values[
            piece * height : (piece + 1) * height
        ]


def front_kernel(
    side_ref,
    seats_ref,
    own_ref,
    other_ref,
    gain_own_ref,
    gain_other_ref,
    wx_ref,
    wz_ref,
    conv_ref,
    bias_ref,
    qw_ref,
    kw_ref,
    vw_ref,
    gate_ref,
    normed_ref,
    flipped_ref,
    upx_ref,
    upz_ref,
    conv_out_ref,
    slope_ref,
    q_ref,
    k_ref,
    v_ref,
    gates_ref,
    padded_ref,
):
    step = pl.program_id(0)
    side = side_ref[0]
    length, part = own_ref.shape
    tap_count = conv_ref.shape[0]

    @pl.when(step == 0)
    def _():
        for start in range(0, length, block):
            rows = pl.ds(start, block)
            own = own_ref[rows, :].astype(f32)
            other = other_ref[rows, :].astype(f32)
            center, scale = row_stats(own, other)
            normed_ref[rows, side_cols(side, part)] = (
                (own - center) * scale * gain_own_ref[...].astype(f32)
            ).astype(b16)
            normed_ref[rows, side_cols(1 - side, part)] = (
                (other - center) * scale * gain_other_ref[...].astype(f32)
            ).astype(b16)
        gates_ref[...] = jnp.zeros_like(gates_ref)
        padded_ref[pl.ds(0, 8), :] = jnp.zeros((8, group), f32)

    flip_rows = flipped_ref.shape[1]
    flat = normed_ref[pl.ds(pl.multiple_of(step * flip_rows, flip_rows), flip_rows), :].T
    seat_rows(flat, seats_ref, flipped_ref)
    upz_ref[...] = dot_nn(normed_ref[...], wz_ref[...]).astype(b16)
    upx = dot_nn(normed_ref[...], wx_ref[...])
    upx_b = upx.astype(b16)
    upx_ref[...] = upx_b
    padded_ref[pl.ds(8, length), :] = upx
    taps = conv_ref[...].astype(f32)
    pre = bias_ref[...].astype(f32) + taps[tap_count - 1 : tap_count] * upx
    for tap in range(tap_count - 1):
        pre = pre + taps[tap : tap + 1] * padded_ref[pl.ds(8 - (tap_count - 1 - tap), length), :]
    gate = sigmoid(pre)
    conv_out = pre * gate
    conv_b = conv_out.astype(b16)
    conv_out_ref[...] = conv_b
    slope_ref[...] = (gate + conv_out * (1.0 - gate)).astype(b16)
    conv_low = (conv_out - conv_b.astype(f32)).astype(b16)
    upx_low = (upx - upx_b.astype(f32)).astype(b16)
    qd, kd, vd = spread_taps(qw_ref[...]), spread_taps(kw_ref[...]), spread_taps(vw_ref[...])
    q_b = (dot_nn(conv_b, qd) + dot_nn(conv_low, qd)).astype(b16)
    k_b = (dot_nn(conv_b, kd) + dot_nn(conv_low, kd)).astype(b16)
    v_b = (dot_nn(upx_b, vd) + dot_nn(upx_low, vd)).astype(b16)
    q_ref[...] = q_b
    k_ref[...] = k_b
    v_ref[...] = v_b
    gates_ref[...] += (
        dot_nt(gate_ref[0], q_b) + dot_nt(gate_ref[1], k_b) + dot_nt(gate_ref[2], v_b)
    )


def front(side, seats, own, other, gain_own, gain_other, wx, wz, conv, bias, qw, kw, vw, gate):
    length, part = own.shape
    width, channels = wx.shape
    steps = channels // group
    taps = conv.shape[0]
    gate_count = gate.shape[1]

    def columns(rows):
        return spec((rows, group), lambda c: (0, c))

    full = shape_of((length, channels), b16)
    return pl.pallas_call(
        front_kernel,
        grid=(steps,),
        in_specs=[
            smem(),
            smem(),
            whole((length, part)),
            whole((length, part)),
            whole((1, part)),
            whole((1, part)),
            columns(width),
            columns(width),
            columns(taps),
            columns(1),
            columns(taps),
            columns(taps),
            columns(taps),
            spec((3, gate_count, group), lambda c: (0, 0, c)),
        ],
        out_specs=[
            whole((length, width)),
            spec((width, length // steps), lambda c: (0, c)),
            columns(length),
            columns(length),
            columns(length),
            columns(length),
            columns(length),
            columns(length),
            columns(length),
            whole((gate_count, length)),
        ],
        out_shape=[
            shape_of((length, width), b16),
            shape_of((width, length), b16),
            full,
            full,
            full,
            full,
            full,
            full,
            full,
            shape_of((gate_count, length), f32),
        ],
        scratch_shapes=[pltpu.VMEM((length + 8, group), f32)],
        compiler_params=settings(56),
        cost_estimate=cost(19),
        name="front",
    )(side, seats, own, other, gain_own, gain_other, wx, wz, conv, bias, qw, kw, vw, gate)


def scan_lanes(values, combine, empty, reverse=False):
    length = values.shape[1]
    lane = lax.broadcasted_iota(jnp.int32, values.shape, 1)
    distance = 1
    while distance < length:
        if reverse:
            moved = pltpu.roll(values, length - distance, 1)
            inside = lane < length - distance
        else:
            moved = pltpu.roll(values, distance, 1)
            inside = lane >= distance
        values = combine(values, jnp.where(inside, moved, empty))
        distance *= 2
    return values


def pick(side, first, second):
    return jnp.where(side == 0, first, second)


def fold_rows(values):
    rows, lanes = values.shape
    return jnp.sum(values.reshape(rows // 8, 8, lanes), axis=0)


def cell_kernel(
    head_dim,
    side_ref,
    seats_ref,
    forget_ref,
    gates_own_ref,
    gates_other_ref,
    q_ref,
    k_ref,
    v_ref,
    conv_ref,
    upz_ref,
    cot_own_ref,
    cot_other_ref,
    wd_ref,
    gain_ref,
    skip_ref,
    flipped_ref,
    rows_ref,
    keep_ref,
    send_ref,
    dnum_ref,
    skip_grad_ref,
    upz_grad_ref,
    first_ref,
    second_ref,
    gains_ref,
    cols_ref,
    gated_t_ref,
    state_ref,
    gated_ref,
    num_ref,
    den_ref,
    slack_ref,
    sums_ref,
):
    step = pl.program_id(0)
    side = side_ref[0]
    length, channels = q_ref.shape
    heads = channels // head_dim
    gate_count = gates_own_ref.shape[0]
    all_heads = gate_count // 2
    part = cot_own_ref.shape[1]

    @pl.when(step == 0)
    def _():
        gates = gates_own_ref[...] + gates_other_ref[...]
        inlet = pick(side, gates[:heads], gates[heads : 2 * heads])
        forget = pick(
            side, gates[all_heads : all_heads + heads], gates[all_heads + heads : gate_count]
        )
        forget = forget + jnp.concatenate(
            [jnp.full((1, length), forget_ref[side * heads + h], f32) for h in range(heads)], axis=0
        )
        log_forget = jnp.minimum(forget, 0.0) - jnp.log1p(jnp.exp(-jnp.abs(forget)))
        total = scan_lanes(log_forget, jnp.add, 0.0)
        ahead = inlet - total
        top = scan_lanes(jnp.maximum(ahead, 0.0), jnp.maximum, 0.0)
        floor = jnp.exp(-(total + top))
        rows_ref[...] = jnp.concatenate(
            [ahead + jnp.log(f32(head_dim**-0.5)), top, forget, jnp.zeros_like(top)], axis=0
        )
        cols_ref[...] = jnp.concatenate([top, floor, top, floor], axis=0).T
        sums_ref[...] = jnp.zeros_like(sums_ref)

    here = pl.ds(pl.multiple_of(step * block, block), block)

    ones = jnp.ones((length, 128), b16)

    def attend(count):
        span = count * block
        here = pl.ds(span - block, block)
        pieces = []
        for h in range(heads):
            lanes = pl.ds(h * head_dim, head_dim)
            start = span - block
            top = cols_ref[pl.ds(start, block), h : h + 1]
            scores = dot_nt(q_ref[pl.ds(start, block), lanes], k_ref[pl.ds(0, span), lanes])
            done = []
            for piece in range(count):
                there = slice(piece * block, (piece + 1) * block)
                exponent = rows_ref[h : h + 1, there] - top
                if piece == count - 1:
                    row_ids = lax.broadcasted_iota(jnp.int32, (block, block), 0)
                    col_ids = lax.broadcasted_iota(jnp.int32, (block, block), 1)
                    exponent = jnp.where(row_ids >= col_ids, exponent, -jnp.inf)
                done.append((scores[:, there] * jnp.exp(exponent)).astype(b16))
            pieces.append(jnp.concatenate(done, axis=1))
        for h in range(heads):
            lanes = pl.ds(h * head_dim, head_dim)
            num_ref[:, lanes] = dot_nn(pieces[h], v_ref[pl.ds(0, span), lanes])
            den_ref[:, pl.ds(h * 128, 128)] = dot_nn(pieces[h], ones[:span])
        state_ref[...] = dot_nt(cot_own_ref[here, :], wd_ref[:, side_cols(side, part)]) + dot_nt(
            cot_other_ref[here, :], wd_ref[:, side_cols(1 - side, part)]
        )

        small = 64
        floors = cols_ref[here, heads : 2 * heads]

        def tiles():
            for h in range(heads):
                for start in range(0, block, small):
                    yield h, start, pl.ds(start, small), pl.ds(h * head_dim, head_dim)

        stats = {}
        for h, start, rows, lanes in tiles():
            denominator = den_ref[rows, h * 128 : h * 128 + 1]
            floor = floors[start : start + small, h : h + 1]
            inverse = 1.0 / jnp.maximum(jnp.abs(denominator), floor)
            hidden = num_ref[rows, lanes] * inverse
            num_ref[rows, lanes] = hidden
            stats[h, start] = [
                inverse,
                jnp.where(jnp.abs(denominator) >= floor, jnp.where(denominator >= 0.0, inverse, -inverse), 0.0),
                jnp.mean(hidden, axis=1, keepdims=True),
            ]
        for h, start, rows, lanes in tiles():
            centered = num_ref[rows, lanes] - stats[h, start][2]
            num_ref[rows, lanes] = centered
            stats[h, start].append(
                lax.rsqrt(jnp.mean(centered * centered, axis=1, keepdims=True) + eps_norm)
            )
        gain_sums = [jnp.zeros((8, head_dim), f32)] * heads
        skip_sums = [jnp.zeros((8, head_dim), f32)] * heads
        for h, start, rows, lanes in tiles():
            gain = gain_ref[:, lanes].astype(f32)
            skip = skip_ref[:, lanes].astype(f32)
            unit = num_ref[rows, lanes] * stats[h, start][3]
            num_ref[rows, lanes] = unit
            conv_out = conv_ref[rows, lanes].astype(f32)
            inner = unit * gain + skip * conv_out
            upz = upz_ref[rows, lanes].astype(f32)
            gate = sigmoid(upz)
            active = upz * gate
            gated_ref[rows, lanes] = (inner * active).astype(b16)
            grad_state = state_ref[rows, lanes]
            grad_inner = grad_state * active
            upz_grad_ref[pl.ds(span - block + start, small), lanes] = (
                grad_state * inner * (gate + active * (1.0 - gate))
            ).astype(b16)
            skip_grad_ref[rows, lanes] = (grad_inner * skip).astype(b16)
            along = grad_inner * unit
            gain_sums[h] = gain_sums[h] + fold_rows(along)
            skip_sums[h] = skip_sums[h] + fold_rows(grad_inner * conv_out)
            grad_unit = grad_inner * gain
            state_ref[rows, lanes] = grad_unit
            stats[h, start] += [
                jnp.mean(grad_unit, axis=1, keepdims=True),
                jnp.mean(along * gain, axis=1, keepdims=True),
            ]
        for h, start, rows, lanes in tiles():
            inverse, signed, _, scale, mean, moment = stats[h, start]
            dnum_ref[rows, lanes] = (
                (state_ref[rows, lanes] - mean - num_ref[rows, lanes] * moment) * (scale * inverse)
            ).astype(b16)
            slack = -signed * moment * (head_dim * eps_norm) * scale * scale
            slack_ref[rows, pl.ds(h * 128, 128)] = jnp.broadcast_to(slack, (small, 128))
        for h in range(heads):
            lanes = pl.ds(h * head_dim, head_dim)
            sums_ref[0:8, lanes] += gain_sums[h]
            sums_ref[8:16, lanes] += skip_sums[h]
        for h in range(heads):
            rows_ref[3 * heads + h : 3 * heads + h + 1, here] = slack_ref[:, pl.ds(h * 128, 128)].T[0:1]
        gated = gated_ref[...]
        keep_ref[...] = dot_nn(gated, wd_ref[:, side_cols(side, part)]).astype(b16)
        send_ref[...] = dot_nn(gated, wd_ref[:, side_cols(1 - side, part)]).astype(b16)
        seat_rows(gated.T, seats_ref, gated_t_ref.at[:, here])


    for count in range(1, length // block + 1):
        pl.when(step == count - 1)(partial(attend, count))

    @pl.when(step == pl.num_programs(0) - 1)
    def _():
        gains_ref[0:1, :] = jnp.sum(sums_ref[0:8, :], axis=0, keepdims=True)
        gains_ref[1:2, :] = jnp.sum(sums_ref[8:16, :], axis=0, keepdims=True)
        gains_ref[2:8, :] = jnp.zeros((6, channels), f32)
        half = first_ref.shape[0]
        width = 2 * part
        for start in range(0, 2 * half, block):
            out_ref = (first_ref if start < half else second_ref).at[pl.ds(start % half, block), :]
            rows = pl.ds(start, block)
            turned = gated_t_ref[rows, :]
            out_ref[:, side_cols(side, part)] = dot_nn(turned, cot_own_ref[...]).astype(b16)
            out_ref[:, side_cols(1 - side, part)] = dot_nn(turned, cot_other_ref[...]).astype(b16)
            out_ref[:, pl.ds(width, channels)] = dot_nn(
                flipped_ref[rows, :], upz_grad_ref[...]
            ).astype(b16)


def cell(
    side, seats, forget, gates_own, gates_other, q, k, v, conv, upz, cot_own, cot_other, wd, gain,
    skip, flipped, head_dim,
):
    length, channels = q.shape
    part = cot_own.shape[1]
    width = wd.shape[1]
    gate_count = gates_own.shape[0]
    heads = channels // head_dim

    def rows(cols):
        return spec((block, cols), lambda r: (r, 0))

    return pl.pallas_call(
        partial(cell_kernel, head_dim),
        grid=(length // block,),
        in_specs=[
            smem(),
            smem(),
            smem(),
            whole((gate_count, length)),
            whole((gate_count, length)),
            whole((length, channels)),
            whole((length, channels)),
            whole((length, channels)),
            rows(channels),
            rows(channels),
            whole((length, part)),
            whole((length, part)),
            whole((channels, width)),
            whole((1, channels)),
            whole((1, channels)),
            whole((width, length)),
        ],
        out_specs=[
            whole((8, length)),
            rows(part),
            rows(part),
            rows(channels),
            rows(channels),
            whole((length, channels)),
            whole((channels // 2, width + channels)),
            whole((channels // 2, width + channels)),
            whole((8, channels)),
        ],
        out_shape=[
            shape_of((8, length), f32),
            shape_of((length, part), b16),
            shape_of((length, part), b16),
            shape_of((length, channels), b16),
            shape_of((length, channels), b16),
            shape_of((length, channels), b16),
            shape_of((channels // 2, width + channels), b16),
            shape_of((channels // 2, width + channels), b16),
            shape_of((8, channels), f32),
        ],
        scratch_shapes=[
            pltpu.VMEM((length, 8), f32),
            pltpu.VMEM((channels, length), b16),
            pltpu.VMEM((block, channels), f32),
            pltpu.VMEM((block, channels), b16),
            pltpu.VMEM((block, channels), f32),
            pltpu.VMEM((block, heads * 128), f32),
            pltpu.VMEM((block, heads * 128), f32),
            pltpu.VMEM((16, channels), f32),
        ],
        compiler_params=settings(56),
        cost_estimate=cost(25),
        name="cell",
    )(side, seats, forget, gates_own, gates_other, q, k, v, conv, upz, cot_own, cot_other, wd,
      gain, skip, flipped)


def cell_back_kernel(
    h, heads, q_ref, k_ref, v_ref, dnum_ref, rows_ref, prior_ref, dq_ref, dk_ref, dv_ref, gates_ref, cols_ref,
    dk_acc, dv_acc, pair_ref,
):
    length, head_dim = q_ref.shape
    cols_ref[...] = rows_ref[...].T
    gates_ref[...] = prior_ref[...]
    ahead = cols_ref[:, h : h + 1]
    row_ids = lax.broadcasted_iota(jnp.int32, (block, block), 0)
    col_ids = lax.broadcasted_iota(jnp.int32, (block, block), 1)
    blocks = length // block
    for t in range(blocks):
        here = pl.ds(t * block, block)
        top = rows_ref[pl.ds(heads + h, 1), here]
        slack = rows_ref[pl.ds(3 * heads + h, 1), here]
        queries = q_ref[here, :]
        dnum = dnum_ref[here, :]
        for s in range(t + 1):
            there = pl.ds(s * block, block)
            keys = k_ref[there, :]
            exponent = ahead[s * block : (s + 1) * block] - top
            if s == t:
                exponent = jnp.where(row_ids <= col_ids, exponent, -jnp.inf)
            weight = jnp.exp(exponent)
            scores = dot_nt(keys, queries) * weight
            grads = (dot_nt(v_ref[there, :], dnum) + slack) * weight
            grads_b = grads.astype(b16)
            dv_part = dot_nn(scores.astype(b16), dnum)
            dk_part = dot_nn(grads_b, queries)
            dq_part = dot_tn(grads_b, keys)
            if s == t:
                dv_acc[there, :] = dv_part
                dk_acc[there, :] = dk_part
            else:
                dv_acc[there, :] += dv_part
                dk_acc[there, :] += dk_part
            dq = dq_part if s == 0 else dq + dq_part
        dq_ref[here, :] = dq.astype(b16)
        pair_ref[here, 0:128] = jnp.broadcast_to(
            jnp.sum(dq * queries.astype(f32), axis=1, keepdims=True), (block, 128)
        )
    for s in range(blocks):
        there = pl.ds(s * block, block)
        dk = dk_acc[there, :]
        dk_ref[there, :] = dk.astype(b16)
        dv_ref[there, :] = dv_acc[there, :].astype(b16)
        pair_ref[there, 128:256] = jnp.broadcast_to(
            jnp.sum(dk * k_ref[there, :].astype(f32), axis=1, keepdims=True), (block, 128)
        )
    outward = pair_ref[:, 0:128].T[0:1]
    inward = pair_ref[:, 128:256].T[0:1]
    forget = rows_ref[pl.ds(2 * heads + h, 1), :]
    grad_log = scan_lanes(jnp.broadcast_to(outward - inward, (8, length)), jnp.add, 0.0, True)[0:1]
    gates_ref[pl.ds(h, 1), :] = inward
    gates_ref[pl.ds(heads + h, 1), :] = grad_log * sigmoid(-forget)


def cell_back(q, k, v, dnum, rows, prior, h, head_dim):
    length, channels = q.shape
    heads = channels // head_dim
    per_head = spec((length, head_dim), lambda _: (0, h))
    result = whole((length, head_dim))
    full = shape_of((length, head_dim), b16)
    return pl.pallas_call(
        partial(cell_back_kernel, h, heads),
        grid=(1,),
        in_specs=[per_head] * 4 + [whole((8, length))] * 2,
        out_specs=[result, result, result, whole((8, length))],
        out_shape=[full, full, full, shape_of((8, length), f32)],
        scratch_shapes=[
            pltpu.VMEM((length, 8), f32),
            pltpu.VMEM((length, head_dim), f32),
            pltpu.VMEM((length, head_dim), f32),
            pltpu.VMEM((length, 256), f32),
        ],
        compiler_params=settings(56),
        cost_estimate=cost(8),
        name="cell_back",
    )(q, k, v, dnum, rows, prior)


def steps_width(ref):
    return ref.shape[1]


def front_back_kernel(
    heads,
    index,
    reseat,
    side_ref,
    table_ref,
    gates_own_ref,
    gates_other_ref,
    dq_ref,
    dk_ref,
    dv_ref,
    q_ref,
    k_ref,
    v_ref,
    conv_out_ref,
    slope_ref,
    upx_ref,
    skip_grad_ref,
    conv_ref,
    qw_ref,
    kw_ref,
    vw_ref,
    gate_ref,
    flipped_ref,
    *refs,
):
    last = index == heads - 1
    if last:
        gains_ref, *refs = refs
        prior_refs, refs = refs[:index], refs[index:]
    upx_grad_ref, first_ref, second_ref, small_ref, gates_ref, gates_t_ref, padded_ref = refs[:7]
    step = pl.program_id(0)
    side = side_ref[0]
    length = q_ref.shape[0]
    tap_count = conv_ref.shape[0]

    @pl.when(step == 0)
    def _():
        own = gates_own_ref[...]
        other = gates_other_ref[...]
        gates = jnp.concatenate(
            [
                pick(side, own[:heads], other[:heads]),
                pick(side, other[:heads], own[:heads]),
                pick(side, own[heads : 2 * heads], other[heads : 2 * heads]),
                pick(side, other[heads : 2 * heads], own[heads : 2 * heads]),
            ],
            axis=0,
        )
        gates_ref[...] = gates
        gates_t_ref[...] = gates.T
        padded_ref[pl.ds(length, 8), :] = jnp.zeros((8, group), f32)

    gates = gates_ref[...]
    gates_b = gates.astype(b16)
    gates_t = gates_t_ref[...].astype(b16)
    dq_b = (dq_ref[...].astype(f32) + dot_nn(gates_t, gate_ref[0])).astype(b16)
    dk_b = (dk_ref[...].astype(f32) + dot_nn(gates_t, gate_ref[1])).astype(b16)
    dv_b = (dv_ref[...].astype(f32) + dot_nn(gates_t, gate_ref[2])).astype(b16)
    conv_out = conv_out_ref[...]
    upx_b = upx_ref[...]
    grad_conv = (
        skip_grad_ref[...].astype(f32)
        + dot_nt(dq_b, spread_taps(qw_ref[...]))
        + dot_nt(dk_b, spread_taps(kw_ref[...]))
    )
    grad_pre = grad_conv * slope_ref[...].astype(f32)
    padded_ref[pl.ds(0, length), :] = grad_pre
    taps = conv_ref[...].astype(f32)
    upx = upx_b.astype(f32)
    grad_upx = dot_nt(dv_b, spread_taps(vw_ref[...])) + taps[tap_count - 1 : tap_count] * grad_pre
    tap_grads = [jnp.sum(upx * grad_pre, axis=0, keepdims=True)]
    for tap in range(tap_count - 2, -1, -1):
        moved = padded_ref[pl.ds(tap_count - 1 - tap, length), :]
        grad_upx = grad_upx + taps[tap : tap + 1] * moved
        tap_grads.insert(0, jnp.sum(upx * moved, axis=0, keepdims=True))
    grad_b = grad_upx.astype(b16)
    upx_grad_ref[...] = grad_b
    half = first_ref.shape[0]
    height = half // len(reseat)
    for start, out_ref in ((0, first_ref), (half, second_ref)):
        result = dot_nn(flipped_ref[pl.ds(start, half), :], grad_b).astype(b16)
        for seat, source in enumerate(reseat):
            out_ref[
                seat * height : (seat + 1) * height,
                pl.ds(pl.multiple_of(step * group, group), group),
            ] = result[source * height : (source + 1) * height]
    small_ref[:, pl.ds(pl.multiple_of(step * group, group), group)] = jnp.concatenate(
        tap_grads
        + [
            gather_taps(dot_tn(conv_out, dq_b), tap_count),
            gather_taps(dot_tn(conv_out, dk_b), tap_count),
            gather_taps(dot_tn(upx_b, dv_b), tap_count),
            dot_nn(gates_b, q_ref[...]),
            dot_nn(gates_b, k_ref[...]),
            dot_nn(gates_b, v_ref[...]),
            jnp.broadcast_to(jnp.sum(gates, axis=1, keepdims=True), (gates.shape[0], group)),
            jnp.sum(grad_pre, axis=0, keepdims=True),
            jnp.zeros((7, group), f32),
        ],
        axis=0,
    )
    if last:

        @pl.when(step == pl.num_programs(0) - 1)
        def _():
            turned_ref = refs[7]
            small = jnp.concatenate([ref[...] for ref in (*prior_refs, small_ref)], axis=1)
            split = 4 * tap_count + 3 * gates.shape[0]
            stacked = jnp.concatenate(
                [
                    small[:split],
                    small[split + gates.shape[0] : split + gates.shape[0] + 1],
                    gains_ref[0:2, :],
                    jnp.zeros((128 - split - 3, small.shape[1]), f32),
                ],
                axis=0,
            )
            turned_ref[...] = stacked.T
            span = steps_width(small_ref)
            for seat in range(2 * len(reseat)):
                out_ref = first_ref if seat < len(reseat) else second_ref
                start = seat % len(reseat) * height
                out_ref[start : start + height, span : span + 128] = turned_ref[
                    pl.ds(pl.multiple_of(table_ref[seat] * height, height), height), :
                ].astype(b16)


def front_back(
    side, table, gates_own, gates_other, dq, dk, dv, q, k, v, conv_out, slope, upx, skip_grad, conv,
    qw, kw, vw, gate, flipped, gains, priors, heads, index, reseat,
):
    length, channels = q.shape
    width = flipped.shape[0]
    taps = conv.shape[0]
    gate_count = gate.shape[1]
    parts = heads
    steps = channels // group // parts
    base = index * steps
    last = index == heads - 1
    out_width = channels // parts + (128 if last else 0)
    extra = [gains, *priors] if last else []
    scratch = [pltpu.VMEM((channels, 128), f32)] if last else []

    def columns(rows):
        return spec((rows, group), lambda c: (0, base + c))

    def results(rows):
        return spec((rows, group), lambda c: (0, c))

    return pl.pallas_call(
        partial(front_back_kernel, heads, index, reseat),
        grid=(steps,),
        in_specs=[smem(), smem(), whole((8, length)), whole((8, length))]
        + [results(length)] * 3
        + [columns(length)] * 7
        + [columns(taps)] * 4
        + [spec((3, gate_count, group), lambda c: (0, 0, base + c)), whole((width, length))]
        + [whole(value.shape) for value in extra],
        out_specs=[
            results(length),
            whole((width // 2, out_width)),
            whole((width // 2, out_width)),
            whole((56, channels // parts)),
        ],
        out_shape=[
            shape_of((length, channels // parts), b16),
            shape_of((width // 2, out_width), b16),
            shape_of((width // 2, out_width), b16),
            shape_of((56, channels // parts), f32),
        ],
        scratch_shapes=[
            pltpu.VMEM((gate_count, length), f32),
            pltpu.VMEM((length, gate_count), f32),
            pltpu.VMEM((length + 8, group), f32),
        ]
        + scratch,
        compiler_params=settings(56),
        cost_estimate=cost(8),
        name="front_back",
    )(side, table, gates_own, gates_other, dq, dk, dv, q, k, v, conv_out, slope, upx, skip_grad, conv,
      qw, kw, vw, gate, flipped, *extra)


def norm_back_kernel(
    parts,
    side_ref,
    *refs,
):
    upx_grad_refs = refs[:parts]
    norm_back_body(side_ref, upx_grad_refs, *refs[parts:])


def norm_back_body(
    side_ref,
    upx_grad_refs,
    upz_grad_ref,
    wx_ref,
    wz_ref,
    own_ref,
    other_ref,
    gain_own_ref,
    gain_other_ref,
    keep_ref,
    send_ref,
    stats_ref,
    gains_ref,
):
    step = pl.program_id(0)
    side = side_ref[0]
    part = own_ref.shape[1]

    @pl.when(step == 0)
    def _():
        gains_ref[...] = jnp.zeros_like(gains_ref)

    own = own_ref[...].astype(f32)
    other = other_ref[...].astype(f32)
    center, scale = row_stats(own, other)
    sums = []
    for index, (values, place, gain_ref, out_ref) in enumerate(
        [(own, side, gain_own_ref, keep_ref), (other, 1 - side, gain_other_ref, send_ref)]
    ):
        rows = side_cols(place, part)
        terms = dot_nt(upz_grad_ref[...], wz_ref[rows, :])
        for index_part, grad_ref in enumerate(upx_grad_refs):
            span = grad_ref.shape[1]
            lanes = pl.ds(index_part * span, span)
            terms = terms + dot_nt(grad_ref[...], wx_ref[rows, lanes])
        out_ref[...] = terms.astype(b16)
        unit = (values - center) * scale
        along = terms * unit
        gains_ref[index : index + 1, :] += jnp.sum(along, axis=0, keepdims=True)
        gain = gain_ref[...].astype(f32)
        sums.append(
            (
                jnp.sum(terms * gain, axis=1, keepdims=True),
                jnp.sum(along * gain, axis=1, keepdims=True),
            )
        )
    flat = jnp.concatenate(
        [
            jnp.broadcast_to(sums[0][0] + sums[1][0], (block, 128)).T[0:1],
            jnp.broadcast_to(sums[0][1] + sums[1][1], (block, 128)).T[0:1],
            jnp.zeros((6, block), f32),
        ],
        axis=0,
    )
    stats_ref[...] = flat


def norm_back(side, upx_grads, upz_grad, wx, wz, own, other, gain_own, gain_other):
    length, channels = upz_grad.shape
    parts = len(upx_grads)
    part = own.shape[1]
    width = wx.shape[0]

    def rows(cols):
        return spec((block, cols), lambda r: (r, 0))

    return pl.pallas_call(
        partial(norm_back_kernel, parts),
        grid=(length // block,),
        in_specs=[smem()]
        + [rows(channels // parts)] * parts
        + [
            rows(channels),
            whole((width, channels)),
            whole((width, channels)),
            rows(part),
            rows(part),
            whole((1, part)),
            whole((1, part)),
        ],
        out_specs=[rows(part), rows(part), spec((8, block), lambda r: (0, r)), whole((8, part))],
        out_shape=[
            shape_of((length, part), b16),
            shape_of((length, part), b16),
            shape_of((8, length), f32),
            shape_of((8, part), f32),
        ],
        compiler_params=settings(56),
        cost_estimate=cost(10),
        name="norm_back",
    )(side, *upx_grads, upz_grad, wx, wz, own, other, gain_own, gain_other)


def seat_back(table_ref, near_ref, far_ref, out_ref):
    pieces = table_ref.shape[0]
    height = out_ref.shape[0] // pieces
    for seat in range(pieces):
        source = near_ref if seat < pieces // 2 else far_ref
        start = seat % (pieces // 2) * height
        out_ref[pl.ds(pl.multiple_of(table_ref[seat] * height, height), height), :] = source[
            start : start + height, :
        ].astype(f32)


def place_rows(table, pair):
    near, far = pair
    half, width = near.shape
    source = spec((half, group), lambda c: (0, c))
    return pl.pallas_call(
        seat_back,
        grid=(width // group,),
        in_specs=[smem(), source, source],
        out_specs=spec((2 * half, group), lambda c: (0, c)),
        out_shape=shape_of((2 * half, width), f32),
        compiler_params=settings(24),
        cost_estimate=cost(3),
        name="place_rows",
    )(table, near, far)


def place_last_kernel(
    taps, gate_count, mixed_ref, far_table_ref, near_ref, far_ref, near_two_ref, far_two_ref,
    near_small_ref, far_small_ref, out_ref, conv_ref, q_ref, k_ref, v_ref, bias_ref, gain_ref,
    skip_ref, gate_ref, turned_ref,
):
    step = pl.program_id(0)
    middle = pl.num_programs(0) // 2

    @pl.when(step == 0)
    def _():
        seat_back(far_table_ref, near_small_ref, far_small_ref, turned_ref)
        flat = turned_ref[...].T
        for at, ref in enumerate((conv_ref, q_ref, k_ref, v_ref)):
            ref[...] = flat[at * taps : (at + 1) * taps]
        start = 4 * taps
        for part in range(3):
            gate_ref[part, :, :] = turned_ref[
                :, start + part * gate_count : start + (part + 1) * gate_count
            ]
        start += 3 * gate_count
        for at, ref in enumerate((bias_ref, gain_ref, skip_ref)):
            ref[...] = flat[start + at : start + at + 1]

    @pl.when(step < middle)
    def _():
        seat_back(mixed_ref, near_ref, far_ref, out_ref)

    @pl.when(step >= middle)
    def _():
        seat_back(far_table_ref, near_two_ref, far_two_ref, out_ref)


def place_last(mixed_table, far_table, pair, pair_two, taps, gate_count):
    half, width = pair[0].shape
    steps = width // group
    channels = 2 * half

    def source(first):
        return spec((half, group), lambda c: (0, jnp.clip(c - first, 0, steps - 1)))

    small = spec((half, 128), lambda c: (0, width // 128))
    row = shape_of((1, channels), f32)
    tap_rows = shape_of((taps, channels), f32)
    shapes = [tap_rows] * 4 + [row] * 3 + [shape_of((3, channels, gate_count), f32)]
    return pl.pallas_call(
        partial(place_last_kernel, taps, gate_count),
        grid=(2 * steps,),
        in_specs=[smem(), smem(), source(0), source(0), source(steps), source(steps), small, small],
        out_specs=[spec((2 * half, group), lambda c: (0, c))] + [whole(v.shape) for v in shapes],
        out_shape=[shape_of((2 * half, 2 * width), f32)] + shapes,
        scratch_shapes=[pltpu.VMEM((channels, 128), f32)],
        compiler_params=settings(32),
        cost_estimate=cost(5),
        name="place_last",
    )(mixed_table, far_table, *pair, *pair_two, *pair_two)


def finish_kernel(
    own_ref, other_ref, gain_ref, keep_ref, recv_ref, stats_own_ref, stats_other_ref, cot_ref,
    out_ref,
):
    own = own_ref[...].astype(f32)
    center, scale = row_stats(own, other_ref[...].astype(f32))
    stats = (stats_own_ref[...] + stats_other_ref[...]).T
    width = own.shape[1] + other_ref.shape[1]
    terms = keep_ref[...].astype(f32) + recv_ref[...].astype(f32)
    unit = (own - center) * scale
    pulled = terms * gain_ref[...].astype(f32) - (stats[:, 0:1] + unit * stats[:, 1:2]) / width
    out_ref[...] = cot_ref[...].astype(f32) + pulled * scale


def finish(own, other, gain, keep, recv, stats_own, stats_other, cot):
    length, part = own.shape
    rows = spec((block, part), lambda r: (r, 0))
    stats = spec((8, block), lambda r: (0, r))
    return pl.pallas_call(
        finish_kernel,
        grid=(length // block,),
        in_specs=[rows, rows, whole((1, part)), rows, rows, stats, stats, rows],
        out_specs=rows,
        out_shape=shape_of((length, part), f32),
        compiler_params=settings(32),
        cost_estimate=cost(4),
        name="finish",
    )(own, other, gain, keep, recv, stats_own, stats_other, cot)


def swap(values):
    return lax.ppermute(values, "head", [(0, 1), (1, 0)])


def across(values, bit, count):
    return lax.ppermute(values, "dp", [(i, i ^ (1 << bit)) for i in range(count)])


def add_halves(first, second):
    return (first.astype(f32) + second.astype(f32)).astype(first.dtype)


class Reduction:
    def __init__(self, keep, out, order, bits, count, step=0):
        self.keep, self.out, self.count = keep, out, count
        self.plan = (
            [("half", bit) for bit in order]
            + [("full", bit) for bit in range(len(order), bits)]
            + [("copy", bit) for bit in reversed(order)]
        )
        self.step = step

    def send(self):
        if not self.more():
            return None
        self.got = across(self.keep if self.out is None else self.out, self.plan[self.step][1], self.count)
        return self.got

    def take(self, got=None):
        if not self.more():
            return
        got = self.got if got is None else got
        kind, bit = self.plan[self.step]
        self.step += 1
        after = self.plan[self.step][0] if self.step < len(self.plan) else "end"
        if kind == "copy":
            if after == "end":
                self.result = (self.keep, got)
            else:
                self.keep = jnp.concatenate([self.keep, got], axis=0)
                self.out = None
        elif after == "half":
            half = self.keep.shape[0] // 2
            self.out = add_halves(self.keep[half:], got[half:])
            self.keep = add_halves(self.keep[:half], got[:half])
        else:
            self.keep = add_halves(self.keep, got)
            self.out = None

    def more(self):
        return self.step < len(self.plan)


def arrange(order, place):
    levels = len(order)
    return sum((((place >> bit) & 1) << (levels - 1 - at)) for at, bit in enumerate(order))


def settle(value, *flows):
    flows = [flow for flow in flows if flow.more()]
    value, gots = lax.optimization_barrier((value, [flow.got for flow in flows]))
    for flow, got in zip(flows, gots):
        flow.take(got)
    flows = [flow for flow in flows if flow.more()]
    held = [(flow.keep, flow.out) for flow in flows]
    value, held = lax.optimization_barrier((value, held))
    for flow, (keep, out) in zip(flows, held):
        flow.keep, flow.out = keep, out
    return value


def send_all(flows):
    for flow in flows:
        flow.send()


def on_device(
    layer_input,
    ln_gain,
    up_x_weight,
    up_z_weight,
    conv_weight,
    conv_bias,
    query_weight,
    key_weight,
    value_weight,
    gate_weight,
    forget_bias,
    norm_gain,
    skip_gain,
    down_weight,
    cotangent,
):
    head_index = lax.axis_index("head")
    place = lax.axis_index("dp")
    count = lax.axis_size("dp")
    side = head_index.astype(jnp.int32).reshape(1)
    part = layer_input.shape[1]
    channels = up_x_weight.shape[1]
    all_heads = gate_weight.shape[2] // 2
    heads = all_heads // lax.axis_size("head")
    head_dim = channels // heads
    taps = conv_weight.shape[0]
    bits = count.bit_length() - 1
    levels = min(bits, 3)
    near_order = list(range(levels))
    far_order = near_order[:1] + near_order[2:3] + near_order[1:2] + near_order[3:]
    pieces = 2**levels
    turned = [0] * pieces
    for relative in range(pieces):
        turned[arrange(near_order, relative)] = arrange(far_order, relative)
    seats = jnp.arange(pieces, dtype=jnp.int32)
    near_table = (seats ^ arrange(near_order, place)).astype(jnp.int32)
    far_table = (seats ^ arrange(far_order, place)).astype(jnp.int32)
    mixed_table = (jnp.array(turned, jnp.int32) ^ arrange(far_order, place)).astype(jnp.int32)
    middle = max(pieces // 2, 1)
    straight = list(range(middle))
    mixed = [turned[seat] for seat in range(middle)]

    gain_own = ln_gain.reshape(1, part)
    gain_other = swap(gain_own)
    input_other = swap(layer_input)
    cot_start, input_other, gain_other = lax.optimization_barrier(
        (cotangent, input_other, gain_other)
    )
    cot_other = swap(cot_start)
    gate_t = gate_weight.transpose(0, 2, 1)
    normed, flipped, upx, upz, conv_out, slope, q, k, v, gates = front(
        side, far_table, layer_input, input_other, gain_own, gain_other, up_x_weight, up_z_weight,
        conv_weight, conv_bias.reshape(1, channels), query_weight, key_weight, value_weight, gate_t,
    )
    gates_other = swap(gates)
    rows, keep, send, dnum, skip_grad, upz_grad, early_keep, early_send, gains = cell(
        side, near_table, forget_bias.astype(f32), gates, gates_other, q, k, v, conv_out, upz,
        cotangent, cot_other, down_weight, norm_gain.reshape(1, channels),
        skip_gain.reshape(1, channels), flipped, head_dim,
    )
    width = down_weight.shape[1]
    down_other = swap(send)
    got = across(early_send, near_order[0], count)
    grads = [cell_back(q, k, v, dnum, rows, rows, 0, head_dim)]
    prior, got = lax.optimization_barrier((grads[0][3], got))
    first = Reduction(early_keep[:, :width], None, near_order, bits, count)
    second = Reduction(early_keep[:, width:], None, far_order, bits, count)
    first.got, second.got = got[:, :width], got[:, width:]
    prior = settle(prior, first, second)
    first.send()
    second.send()
    gate_grads = cell_back(q, k, v, dnum, rows, prior, 1, head_dim)
    grads.append(gate_grads)
    gate_grads = settle(gate_grads[3], first, second)
    gate_grads_other = swap(gate_grads)
    first.send()
    second.send()
    late = []
    upx_grads = []
    smalls = []

    def back(index, order, reseat):
        dq, dk, dv, _ = grads[index]
        upx_grad, late_keep, late_send, small = front_back(
            side, far_table, gate_grads, gate_grads_other, dq, dk, dv, q, k, v, conv_out, slope,
            upx, skip_grad, conv_weight, query_weight, key_weight, value_weight, gate_t, flipped,
            gains, list(smalls), heads, index, reseat,
        )
        upx_grads.append(upx_grad)
        smalls.append(small)
        late.append(Reduction(late_keep, late_send, order, bits, count))
        late[-1].send()

    back(0, near_order, mixed)
    layer_output = (
        layer_input.astype(f32) + keep.astype(f32) + down_other.astype(f32)
    ).astype(b16)
    gate_grads_other, layer_output = settle((gate_grads_other, layer_output), first, second)
    send_all([first, second])
    back(1, far_order, straight)
    upx_grads[1] = settle(upx_grads[1], *late)
    send_all(late)
    terms = norm_back(
        side, upx_grads, upz_grad, up_x_weight, up_z_weight, layer_input, input_other, gain_own,
        gain_other,
    )
    flows = [first, second, *late]
    terms_keep, terms_send, stats, ln_parts = settle(terms, *flows)
    stats_other = swap(stats)
    ln_other = swap(ln_parts[1:2])
    terms_other = swap(terms_send)
    send_all(flows)
    stats_other, ln_other = settle((stats_other, ln_other), *flows)
    sums = smalls[0][-12:-8, 0]
    tiny = jnp.concatenate([(ln_parts[0] + ln_other[0]), sums, jnp.zeros((124,), f32)])
    flows.append(Reduction(tiny.reshape(-1, 128), None, [], bits, count))
    send_all(flows)
    settle((), *flows)
    send_all(flows)
    terms_other = settle(terms_other, *flows)
    send_all(flows)
    input_grad = finish(
        layer_input, input_other, gain_own, terms_keep, terms_other, stats, stats_other, cotangent
    )
    input_grad = settle(input_grad, *flows)
    while any(flow.more() for flow in flows):
        send_all(flows)
        settle((), *flows)
    grad_down = place_rows(near_table, first.result)
    grad_upz = place_rows(far_table, second.result)
    grad_upx, conv_grad, q_grad, k_grad, v_grad, bias_grad, gain_grad, skip_sum, gate_grad = (
        place_last(mixed_table, far_table, late[0].result, late[1].result, taps, 2 * all_heads)
    )
    tiny = flows[-1].keep.reshape(-1)
    return (
        layer_output,
        input_grad,
        tiny[:part],
        grad_upx,
        grad_upz,
        conv_grad,
        bias_grad.reshape(-1),
        q_grad,
        k_grad,
        v_grad,
        gate_grad,
        tiny[part : part + all_heads],
        gain_grad.reshape(-1),
        skip_sum.reshape(-1),
        grad_down,
    )


def solution(mesh):
    in_specs = (
        P("dp", "head"),
        P("head"),
        P(None, "head"),
        P(None, "head"),
        P(None, "head"),
        P("head"),
        P(None, "head"),
        P(None, "head"),
        P(None, "head"),
        P(None, "head", None),
        P(),
        P("head"),
        P("head"),
        P("head", None),
        P("dp", "head"),
    )
    out_specs = (
        P("dp", "head"),
        P("dp", "head"),
        P("head"),
        P(None, "head"),
        P(None, "head"),
        P(None, "head"),
        P("head"),
        P(None, "head"),
        P(None, "head"),
        P(None, "head"),
        P(None, "head", None),
        P(),
        P("head"),
        P("head"),
        P("head", None),
    )
    return jax.shard_map(
        on_device, mesh=mesh, in_specs=in_specs, out_specs=out_specs, check_vma=False
    )
```

time: 1150 us -> 239 us (0.21)
  waiting for transfers between devices: 413 us -> 64.7 us
  matrix products: 333 us -> 0 us
  local copies, waits for them, and re-layouts: 199 us -> 10.1 us
  other arithmetic: 146 us -> 7.52 us
  Pallas kernels: 0 us -> 108 us
  starting transfers between devices: 0.41 us -> 43.4 us
  blocking collectives: 20.9 us -> 0 us
  between operations: 16.6 us -> 1.32 us
    psum x3 -> x0, waiting for transfers between devices: 368 us -> none  [the longest x2 336 us: on_device(): lax.psum((grad_ln_gain, grad_upx_weight, grad_upz_weight, grad_conv_weigh...]
    dot_general x54 -> x0, matrix products: 333 us -> none  [the longest x42 280 us: matmul(): jnp.dot(first, second, precision=lax.Precision.HIGHEST, preferred_element...]
    pallas_call x0 -> x11, Pallas kernels: none -> 108 us  [the longest x1 28.2 us: cell(): pl.pallas_call(partial(cell_kernel, head_dim), grid=(length // block,), i...]
    ppermute x0 -> x40, waiting for transfers between devices: none -> 64.7 us  [the longest x31 36.4 us: across(): return lax.ppermute(values, 'dp', [(i, i ^ 1 << bit) for i in range(count)])]
    convert_element_type x14 -> x16, other arithmetic: 57.3 us -> 5.25 us  [the longest x14 3.34 us: add_halves(): return (first.astype(f32) + second.astype(f32)).astype(first.dtype)]
    ppermute x0 -> x40, starting transfers between devices: none -> 43.4 us  [the longest x31 31.3 us: across(): return lax.ppermute(values, 'dp', [(i, i ^ 1 << bit) for i in range(count)])]
    reduce_sum x21 -> x0, other arithmetic: 35.6 us -> none  [the longest x1 13.5 us: blockwise(): running = running + coefficient * jnp.roll(inputs, -offset_shift, axis=1)]
    unnamed x342 -> x51, local copies, waits for them, and re-layouts: 38.1 us -> 4.16 us
  transfers between devices with their start and end apart: 6 -> 40, of which waited for: 5 -> 17; matrix products, arithmetic and copies ran while one was open for 19% -> 5% of each run, Pallas kernels for 0% -> 28%
where the time goes in v1:
time: 239 us; the launch traced here: 235 us
  Pallas kernels  108 us (45%)
  waiting for transfers between devices  64.7 us (27%)
  starting transfers between devices  43.4 us (18%)
  local copies, waits for them, and re-layouts  10.1 us (4%)
  other arithmetic  7.52 us (3%)
    ppermute x31, waiting for transfers between devices, across(): return lax.ppermute(values, 'dp', [(i, i ^ 1 << bit) for i in range(count)])  36.4 us
    ppermute x31, starting transfers between devices, across(): return lax.ppermute(values, 'dp', [(i, i ^ 1 << bit) for i in range(count)])  31.3 us
    ppermute x9, waiting for transfers between devices, swap(): return lax.ppermute(values, 'head', [(0, 1), (1, 0)])  28.3 us
    pallas_call x1, Pallas kernels, cell(): pl.pallas_call(partial(cell_kernel, head_dim), grid=(length // block,), i...  28.2 us
    pallas_call x2, Pallas kernels, front_back(): pl.pallas_call(partial(front_back_kernel, heads, index, reseat), grid=(st...  20.6 us
    pallas_call x1, Pallas kernels, front(): pl.pallas_call(front_kernel, grid=(steps,), in_specs=[smem(), smem(), who...  18.9 us
    pallas_call x2, Pallas kernels, cell_back(): pl.pallas_call(partial(cell_back_kernel, h, heads), grid=(1,), in_specs=[...  16.7 us
    ppermute x9, starting transfers between devices, swap(): return lax.ppermute(values, 'head', [(0, 1), (1, 0)])  12.1 us
  transfers between devices with their start and end apart: 40, of which 17 were waited for; matrix products, arithmetic and copies ran while one was open for 5% of the time, Pallas kernels for 28%

profile of v1, /device:TPU:0, one launch (start us, length us, event | category | flops | bytes accessed | tf_op | source)
XLA Modules:
  0.0 234.8 jit_solution(5844292937946178171)
XLA Ops:
  0.6 3.0 %collective-permute-start = (bf16[1024,512]{1,0:T(8,128)(2,1)}, bf16[1024,512]{1,0:T(8,128)(2,1)S(1)}, u32[]{:S(2)}, u32[]{:S(2)}) collective-permute-start(bf16[1024,512]{1,0:T(8,128)(2,1)} %own_ref.3), channel_id=1, source_target_pairs={{0,1},{1,0},{2,3},{3,2},{4,5},{5,4},{6,7},{7,6},{8,9},{9,8},{10,11... | collective-permute-start | bytes 3145736 | tf_op jit(solution)/shard_map/ppermute | solution.py:1020
  6.2 20.9 %collective-permute-done.1.gain_other_ref.refs_8_ = bf16[1,512]{1,0:T(2,128)(2,1)S(1)} collective-permute-done((bf16[1,512]{1,0:T(2,128)(2,1)S(1)}, bf16[1,512]{1,0:T(2,128)(2,1)S(1)}, u32[]{:S(2)}, u32[]{:S(2)}) %collective-permute-start.1) | collective-permute-done | bytes 1056 | tf_op jit(solution)/shard_map/ppermute | solution.py:1020
  28.9 18.9 %front.1 = (bf16[1024,1024]{1,0:T(8,128)(2,1)}, bf16[1024,1024]{1,0:T(8,128)(2,1)}, bf16[1024,1024]{1,0:T(8,128)(2,1)}, bf16[1024,1024]{1,0:T(8,128)(2,1)}, bf16...) custom-call(s32[1]{0:T(128)} %bitcast.side_ref, ...), custom_call_target="tpu_custom_call" | custom-call | flops 20899999744 | bytes 68400000 | tf_op jit(solution)/shard_map/front/pallas_call | solution.py:195
  53.4 28.2 %cell.1 = (f32[8,1024]{1,0:T(8,128)}, bf16[1024,512]{1,0:T(8,128)(2,1)}, bf16[1024,512]{1,0:T(8,128)(2,1)}, bf16[1024,1024]{1,0:T(8,128)(2,1)}, bf16[1024,1024]{...) custom-call(s32[1]{0:T(128)} %bitcast.side_ref, ...), custom_call_target="tpu_custom_call" | custom-call | flops 27499999232 | bytes 90000000 | tf_op jit(solution)/shard_map/cell/pallas_call | solution.py:473
  83.1 8.3 %cell_back.2 = (bf16[1024,512]{1,0:T(8,128)(2,1)}, bf16[1024,512]{1,0:T(8,128)(2,1)}, bf16[1024,512]{1,0:T(8,128)(2,1)}, f32[8,1024]{1,0:T(8,128)}) custom-call(bf16[1024,1024]{1,0:T(8,128)(2,1)} %get-tuple-element.161.q_ref, bf16[1024,1024]{1,0:T(8,128)(2,1)} %get-tuple-element.162.k_ref, bf16[1024,1024]{1,0:T(8,128)(2,1)} %get-tuple-element.163.v_ref, ...), custom_call_target="tpu_custom_call" | custom-call | flops 8800000000 | bytes 28800000 | tf_op jit(solution)/shard_map/cell_back/pallas_call | solution.py:596
  97.2 8.3 %cell_back.3 = (bf16[1024,512]{1,0:T(8,128)(2,1)}, bf16[1024,512]{1,0:T(8,128)(2,1)}, bf16[1024,512]{1,0:T(8,128)(2,1)}, f32[8,1024]{1,0:T(8,128)}) custom-call(bf16[1024,1024]{1,0:T(8,128)(2,1)} %get-tuple-element.161.q_ref, bf16[1024,1024]{1,0:T(8,128)(2,1)} %get-tuple-element.162.k_ref, bf16[1024,1024]{1,0:T(8,128)(2,1)} %get-tuple-element.163.v_ref, ...), custom_call_target="tpu_custom_call" | custom-call | flops 8800000000 | bytes 28800000 | tf_op jit(solution)/shard_map/cell_back/pallas_call | solution.py:596
  105.5 2.6 %collective-permute-done.5 = bf16[256,1024]{1,0:T(8,128)(2,1)S(1)} collective-permute-done((bf16[256,1024]{1,0:T(8,128)(2,1)S(1)}, bf16[256,1024]{1,0:T(8,128)(2,1)S(1)}, u32[]{:S(2)}, u32[]{:S(2)}) %collective-permute-start.5) | collective-permute-done | bytes 524320 | tf_op jit(solution)/shard_map/ppermute | solution.py:1024
  114.5 10.0 %front_back.2 = (bf16[1024,512]{1,0:T(8,128)(2,1)}, bf16[512,512]{1,0:T(8,128)(2,1)}, bf16[512,512]{1,0:T(8,128)(2,1)}, f32[56,512]{1,0:T(8,128)}) custom-call(s32[1]{0:T(128)} %bitcast.side_ref, s32[8]{0:T(128)} %iota_xor_fusion.1.seats_ref.table_ref.far_table_ref, f32[8,1024]{1,0:T(8,128)} %get-tuple-element.188.gates_own_ref, f32[8,1024]{1,0:T(8,128)} %copy-done.20, ...), custom_call_target="tpu_custom_call" | custom-call | flops 8800000000 | bytes 28800000 | tf_op jit(solution)/shard_map/front_back/pallas_call | solution.py:768
  124.7 10.6 %front_back.3 = (bf16[1024,512]{1,0:T(8,128)(2,1)}, bf16[512,640]{1,0:T(8,128)(2,1)}, bf16[512,640]{1,0:T(8,128)(2,1)}, f32[56,512]{1,0:T(8,128)}) custom-call(s32[1]{0:T(128)} %bitcast.side_ref, s32[8]{0:T(128)} %iota_xor_fusion.1.seats_ref.table_ref.far_table_ref, f32[8,1024]{1,0:T(8,128)} %get-tuple-element.188.gates_own_ref, f32[8,1024]{1,0:T(8,128)} %copy-done.20, ...), custom_call_target="tpu_custom_call" | custom-call | flops 8800000000 | bytes 28800000 | tf_op jit(solution)/shard_map/front_back/pallas_call | solution.py:768
  135.9 2.6 %collective-permute-start.13 = (bf16[128,1024]{1,0:T(8,128)(2,1)S(1)}, bf16[128,1024]{1,0:T(8,128)(2,1)S(1)}, u32[]{:S(2)}, u32[]{:S(2)}) collective-permute-start(bf16[128,1024]{1,0:T(8,128)(2,1)S(1)} %add_convert_fusion.12), channel_id=1, source_target_pairs={{0,16},{2,18},{4,20},{6,22},{8,24},{10,26},{12,28},{14,30},{16,0},... | collective-permute-start | bytes 786440 | tf_op jit(solution)/shard_map/ppermute | solution.py:1024
  142.2 10.0 %norm_back.1 = (bf16[1024,512]{1,0:T(8,128)(2,1)}, bf16[1024,512]{1,0:T(8,128)(2,1)}, f32[8,1024]{1,0:T(8,128)}, f32[8,512]{1,0:T(8,128)}) custom-call(s32[1]{0:T(128)} %bitcast.side_ref, bf16[1024,512]{1,0:T(8,128)(2,1)} %get-tuple-element.206.refs_0_, bf16[1024,512]{1,0:T(8,128)(2,1)} %get-tuple-element.221.refs_1_, ...), custom_call_target="tpu_custom_call" | custom-call | flops 11000000512 | bytes 36000000 | tf_op jit(solution)/shard_map/norm_back/pallas_call | solution.py:878
  152.2 4.9 %collective-permute-done.13 = bf16[128,1024]{1,0:T(8,128)(2,1)S(1)} collective-permute-done((bf16[128,1024]{1,0:T(8,128)(2,1)S(1)}, bf16[128,1024]{1,0:T(8,128)(2,1)S(1)}, u32[]{:S(2)}, u32[]{:S(2)}) %collective-permute-start.13) | collective-permute-done | bytes 262176 | tf_op jit(solution)/shard_map/ppermute | solution.py:1024
  157.2 4.8 %collective-permute-done.14 = bf16[128,1024]{1,0:T(8,128)(2,1)S(1)} collective-permute-done((bf16[128,1024]{1,0:T(8,128)(2,1)S(1)}, bf16[128,1024]{1,0:T(8,128)(2,1)S(1)}, u32[]{:S(2)}, u32[]{:S(2)}) %collective-permute-start.14) | collective-permute-done | bytes 262176 | tf_op jit(solution)/shard_map/ppermute | solution.py:1024
  168.5 2.2 collective-permute-done.19
  172.1 2.5 %collective-permute-done.18.stats_other_ref = f32[8,1024]{1,0:T(8,128)S(1)} collective-permute-done((f32[8,1024]{1,0:T(8,128)S(1)}, f32[8,1024]{1,0:T(8,128)S(1)}, u32[]{:S(2)}, u32[]{:S(2)}) %collective-permute-start.18) | collective-permute-done | bytes 32800 | tf_op jit(solution)/shard_map/ppermute | solution.py:1020
  184.7 7.3 %collective-permute-done.26 = bf16[128,512]{1,0:T(8,128)(2,1)S(1)} collective-permute-done((bf16[128,512]{1,0:T(8,128)(2,1)S(1)}, bf16[128,512]{1,0:T(8,128)(2,1)S(1)}, u32[]{:S(2)}, u32[]{:S(2)}) %collective-permute-start.26) | collective-permute-done | bytes 131104 | tf_op jit(solution)/shard_map/ppermute | solution.py:1024
  197.8 4.2 %collective-permute-done.33 = f32[5,128]{1,0:T(8,128)S(1)} collective-permute-done((f32[5,128]{1,0:T(8,128)S(1)}, f32[5,128]{1,0:T(8,128)S(1)}, u32[]{:S(2)}, u32[]{:S(2)}) %collective-permute-start.33) | collective-permute-done | bytes 2592 | tf_op jit(solution)/shard_map/ppermute | solution.py:1024
  204.2 2.9 %collective-permute-done.31 = bf16[128,512]{1,0:T(8,128)(2,1)S(1)} collective-permute-done((bf16[128,512]{1,0:T(8,128)(2,1)S(1)}, bf16[128,512]{1,0:T(8,128)(2,1)S(1)}, u32[]{:S(2)}, u32[]{:S(2)}) %collective-permute-start.31) | collective-permute-done | bytes 131104 | tf_op jit(solution)/shard_map/ppermute | solution.py:1024
  211.2 3.2 %finish.1 = f32[1024,512]{1,0:T(8,128)} custom-call(bf16[1024,512]{1,0:T(8,128)(2,1)S(1)} %copy-done.1, bf16[1024,512]{1,0:T(8,128)(2,1)S(1)} %copy-done.6, bf16[1,512]{1,0:T(2,128)(2,1)S(1)} %copy-done.3, bf16[1024,512]{1,0:T(8,128)(2,1)S(1)} %copy-done.10, bf16[1024,512]{1,0:T(8,128)(2,1)S(1)} %collective-permute-done.17.recv_ref, ...), custom_call_target="tpu_custom_call" | custom-call | flops 4400000000 | bytes 14400000 | tf_op jit(solution)/shard_map/finish/pallas_call | solution.py:1007
  214.4 2.2 collective-permute-done.34
  219.4 3.1 %place_rows.3 = f32[1024,1024]{1,0:T(8,128)} custom-call(s32[8]{0:T(128)S(1)} %copy-done.9, bf16[512,1024]{1,0:T(8,128)(2,1)S(1)} %pad_maximum_fusion.near_ref, bf16[512,1024]{1,0:T(8,128)(2,1)S(1)} %collective-permute-done.29.far_ref), custom_call_target="tpu_custom_call" | custom-call | flops 3300000000 | bytes 10800000 | tf_op jit(solution)/shard_map/place_rows/pallas_call | solution.py:920
  222.6 2.8 %collective-permute-start.39 = (f32[5,128]{1,0:T(8,128)S(1)}, f32[5,128]{1,0:T(8,128)S(1)}, u32[]{:S(2)}, u32[]{:S(2)}) collective-permute-start(f32[5,128]{1,0:T(8,128)S(1)} %add.144), channel_id=1, source_target_pairs={{0,16},{2,18},{4,20},{6,22},{8,24},{10,26},{12,28},{14,30},{16,0},... | collective-permute-start | bytes 7688 | tf_op jit(solution)/shard_map/ppermute | solution.py:1024
  225.4 3.1 %place_rows.2 = f32[1024,1024]{1,0:T(8,128)} custom-call(s32[8]{0:T(128)S(1)} %copy-done.8, bf16[512,1024]{1,0:T(8,128)(2,1)S(1)} %pad_maximum_fusion.1.near_ref, bf16[512,1024]{1,0:T(8,128)(2,1)S(1)} %collective-permute-done.30.far_ref), custom_call_target="tpu_custom_call" | custom-call | flops 3300000000 | bytes 10800000 | tf_op jit(solution)/shard_map/place_rows/pallas_call | solution.py:920
  229.6 3.9 %place_last.1 = (f32[1024,1024]{1,0:T(8,128)}, f32[4,1024]{1,0:T(4,128)}, f32[4,1024]{1,0:T(4,128)}, f32[4,1024]{1,0:T(4,128)}, f32[4,1024]{1,0:T(4,128)}, /*ind...) custom-call(s32[8]{0:T(128)S(1)} %broadcast_xor_fusion.mixed_ref, ...), custom_call_target="tpu_custom_call" | custom-call | flops 5500000256 | bytes 18000000 | tf_op jit(solution)/shard_map/place_last/pallas_call | solution.py:976
  (161 shorter events, 62.6 us)
Async XLA Ops:
  0.6 26.5 %collective-permute-start = (bf16[1024,512]{1,0:T(8,128)(2,1)}, bf16[1024,512]{1,0:T(8,128)(2,1)S(1)}, u32[]{:S(2)}, u32[]{:S(2)}) collective-permute-start(bf16[1024,512]{1,0:T(8,128)(2,1)} %own_ref.3), channel_id=1, source_target_pairs={{0,1},{1,0},{2,3},{3,2},{4,5},{5,4},{6,7},{7,6},{8,9},{9,8},{10,11... | collective-permute-start | bytes 3145736 | tf_op jit(solution)/shard_map/ppermute | solution.py:1020
  4.4 22.7 %collective-permute-start.1 = (bf16[1,512]{1,0:T(2,128)(2,1)S(1)}, bf16[1,512]{1,0:T(2,128)(2,1)S(1)}, u32[]{:S(2)}, u32[]{:S(2)}) collective-permute-start(bf16[1,512]{1,0:T(2,128)(2,1)S(1)} %reshape.63.gain_own_ref.refs_7_.gain_ref), channel_id=1, source_target_pairs={{0,1},{1,0},{2,3},{3,2},{4,5},{5,4},{6,7},{7,6},{8,9},{9,8},{10,11... | collective-permute-start | bytes 3080 | tf_op jit(solution)/shard_map/ppermute | solution.py:1020
  27.1 25.3 %collective-permute-start.3 = (bf16[1024,512]{1,0:T(8,128)(2,1)}, bf16[1024,512]{1,0:T(8,128)(2,1)S(1)}, u32[]{:S(2)}, u32[]{:S(2)}) collective-permute-start(bf16[1024,512]{1,0:T(8,128)(2,1)} %cot_ref.1), channel_id=1, source_target_pairs={{0,1},{1,0},{2,3},{3,2},{4,5},{5,4},{6,7},{7,6},{8,9},{9,8},{10,11... | collective-permute-start | bytes 3145736 | tf_op jit(solution)/shard_map/ppermute | solution.py:1020
  81.6 9.8 %collective-permute-start.4 = (bf16[512,2048]{1,0:T(8,128)(2,1)}, bf16[512,2048]{1,0:T(8,128)(2,1)S(1)}, u32[]{:S(2)}, u32[]{:S(2)}) collective-permute-start(bf16[512,2048]{1,0:T(8,128)(2,1)} %get-tuple-element.172), channel_id=1, source_target_pairs={{0,2},{2,0},{4,6},{6,4},{8,10},{10,8},{12,14},{14,12},{16,18},{18,... | collective-permute-start | bytes 6291464 | tf_op jit(solution)/shard_map/ppermute | solution.py:1024
  81.7 28.7 %collective-permute-start.8 = (bf16[1024,512]{1,0:T(8,128)(2,1)}, bf16[1024,512]{1,0:T(8,128)(2,1)S(1)}, u32[]{:S(2)}, u32[]{:S(2)}) collective-permute-start(bf16[1024,512]{1,0:T(8,128)(2,1)} %get-tuple-element.190), channel_id=1, source_target_pairs={{0,1},{1,0},{2,3},{3,2},{4,5},{5,4},{6,7},{7,6},{8,9},{9,8},{10,11... | collective-permute-start | bytes 3145736 | tf_op jit(solution)/shard_map/ppermute | solution.py:1020
  94.1 14.1 %collective-permute-start.5 = (bf16[256,1024]{1,0:T(8,128)(2,1)S(1)}, bf16[256,1024]{1,0:T(8,128)(2,1)S(1)}, u32[]{:S(2)}, u32[]{:S(2)}) collective-permute-start(bf16[256,1024]{1,0:T(8,128)(2,1)S(1)} %get-tuple-element.181), channel_id=1, source_target_pairs={{0,4},{2,6},{4,0},{6,2},{8,12},{10,14},{12,8},{14,10},{16,20},{18,... | collective-permute-start | bytes 1572872 | tf_op jit(solution)/shard_map/ppermute | solution.py:1024
  95.6 13.7 %collective-permute-start.6 = (bf16[256,1024]{1,0:T(8,128)(2,1)S(1)}, bf16[256,1024]{1,0:T(8,128)(2,1)S(1)}, u32[]{:S(2)}, u32[]{:S(2)}) collective-permute-start(bf16[256,1024]{1,0:T(8,128)(2,1)S(1)} %get-tuple-element.182), channel_id=1, source_target_pairs={{0,8},{2,10},{4,12},{6,14},{8,0},{10,2},{12,4},{14,6},{16,24},{18,... | collective-permute-start | bytes 1572872 | tf_op jit(solution)/shard_map/ppermute | solution.py:1024
  111.8 12.7 %collective-permute-start.9 = (bf16[128,1024]{1,0:T(8,128)(2,1)S(1)}, bf16[128,1024]{1,0:T(8,128)(2,1)S(1)}, u32[]{:S(2)}, u32[]{:S(2)}) collective-permute-start(bf16[128,1024]{1,0:T(8,128)(2,1)S(1)} %get-tuple-element.191), channel_id=1, source_target_pairs={{0,8},{2,10},{4,12},{6,14},{8,0},{10,2},{12,4},{14,6},{16,24},{18,... | collective-permute-start | bytes 786440 | tf_op jit(solution)/shard_map/ppermute | solution.py:1024
  113.4 11.2 %collective-permute-start.10 = (bf16[128,1024]{1,0:T(8,128)(2,1)S(1)}, bf16[128,1024]{1,0:T(8,128)(2,1)S(1)}, u32[]{:S(2)}, u32[]{:S(2)}) collective-permute-start(bf16[128,1024]{1,0:T(8,128)(2,1)S(1)} %get-tuple-element.192), channel_id=1, source_target_pairs={{0,4},{2,6},{4,0},{6,2},{8,12},{10,14},{12,8},{14,10},{16,20},{18,... | collective-permute-start | bytes 786440 | tf_op jit(solution)/shard_map/ppermute | solution.py:1024
  135.9 21.3 %collective-permute-start.13 = (bf16[128,1024]{1,0:T(8,128)(2,1)S(1)}, bf16[128,1024]{1,0:T(8,128)(2,1)S(1)}, u32[]{:S(2)}, u32[]{:S(2)}) collective-permute-start(bf16[128,1024]{1,0:T(8,128)(2,1)S(1)} %add_convert_fusion.12), channel_id=1, source_target_pairs={{0,16},{2,18},{4,20},{6,22},{8,24},{10,26},{12,28},{14,30},{16,0},... | collective-permute-start | bytes 786440 | tf_op jit(solution)/shard_map/ppermute | solution.py:1024
  138.5 23.5 %collective-permute-start.14 = (bf16[128,1024]{1,0:T(8,128)(2,1)S(1)}, bf16[128,1024]{1,0:T(8,128)(2,1)S(1)}, u32[]{:S(2)}, u32[]{:S(2)}) collective-permute-start(bf16[128,1024]{1,0:T(8,128)(2,1)S(1)} %add_convert_fusion.11), channel_id=1, source_target_pairs={{0,16},{2,18},{4,20},{6,22},{8,24},{10,26},{12,28},{14,30},{16,0},... | collective-permute-start | bytes 786440 | tf_op jit(solution)/shard_map/ppermute | solution.py:1024
  140.2 21.7 %collective-permute-start.15 = (bf16[256,512]{1,0:T(8,128)(2,1)S(1)}, bf16[256,512]{1,0:T(8,128)(2,1)S(1)}, u32[]{:S(2)}, u32[]{:S(2)}) collective-permute-start(bf16[256,512]{1,0:T(8,128)(2,1)S(1)} %get-tuple-element.229), channel_id=1, source_target_pairs={{0,4},{2,6},{4,0},{6,2},{8,12},{10,14},{12,8},{14,10},{16,20},{18,... | collective-permute-start | bytes 786440 | tf_op jit(solution)/shard_map/ppermute | solution.py:1024
  141.8 20.2 %collective-permute-start.16 = (bf16[256,640]{1,0:T(8,128)(2,1)S(1)}, bf16[256,640]{1,0:T(8,128)(2,1)S(1)}, u32[]{:S(2)}, u32[]{:S(2)}) collective-permute-start(bf16[256,640]{1,0:T(8,128)(2,1)S(1)} %get-tuple-element.230), channel_id=1, source_target_pairs={{0,8},{2,10},{4,12},{6,14},{8,0},{10,2},{12,4},{14,6},{16,24},{18,... | collective-permute-start | bytes 983048 | tf_op jit(solution)/shard_map/ppermute | solution.py:1024
  162.3 12.4 %collective-permute-start.20 = (bf16[128,1024]{1,0:T(8,128)(2,1)S(1)}, bf16[128,1024]{1,0:T(8,128)(2,1)S(1)}, u32[]{:S(2)}, u32[]{:S(2)}) collective-permute-start(bf16[128,1024]{1,0:T(8,128)(2,1)S(1)} %add_convert_fusion.8), channel_id=1, source_target_pairs={{0,8},{2,10},{4,12},{6,14},{8,0},{10,2},{12,4},{14,6},{16,24},{18,... | collective-permute-start | bytes 786440 | tf_op jit(solution)/shard_map/ppermute | solution.py:1024
  162.9 11.7 %collective-permute-start.21 = (bf16[128,1024]{1,0:T(8,128)(2,1)S(1)}, bf16[128,1024]{1,0:T(8,128)(2,1)S(1)}, u32[]{:S(2)}, u32[]{:S(2)}) collective-permute-start(bf16[128,1024]{1,0:T(8,128)(2,1)S(1)} %add_convert_fusion.7), channel_id=1, source_target_pairs={{0,4},{2,6},{4,0},{6,2},{8,12},{10,14},{12,8},{14,10},{16,20},{18,... | collective-permute-start | bytes 786440 | tf_op jit(solution)/shard_map/ppermute | solution.py:1024
  163.8 10.8 %collective-permute-start.23 = (bf16[128,640]{1,0:T(8,128)(2,1)S(1)}, bf16[128,640]{1,0:T(8,128)(2,1)S(1)}, u32[]{:S(2)}, u32[]{:S(2)}) collective-permute-start(bf16[128,640]{1,0:T(8,128)(2,1)S(1)} %get-tuple-element.248), channel_id=1, source_target_pairs={{0,4},{2,6},{4,0},{6,2},{8,12},{10,14},{12,8},{14,10},{16,20},{18,... | collective-permute-start | bytes 491528 | tf_op jit(solution)/shard_map/ppermute | solution.py:1024
  174.8 18.9 %collective-permute-start.24 = (bf16[256,1024]{1,0:T(8,128)(2,1)S(1)}, bf16[256,1024]{1,0:T(8,128)(2,1)S(1)}, u32[]{:S(2)}, u32[]{:S(2)}) collective-permute-start(bf16[256,1024]{1,0:T(8,128)(2,1)S(1)} %pad_maximum_fusion.3), channel_id=1, source_target_pairs={{0,4},{2,6},{4,0},{6,2},{8,12},{10,14},{12,8},{14,10},{16,20},{18,... | collective-permute-start | bytes 1572872 | tf_op jit(solution)/shard_map/ppermute | solution.py:1024
  176.3 18.6 %collective-permute-start.25 = (bf16[256,1024]{1,0:T(8,128)(2,1)S(1)}, bf16[256,1024]{1,0:T(8,128)(2,1)S(1)}, u32[]{:S(2)}, u32[]{:S(2)}) collective-permute-start(bf16[256,1024]{1,0:T(8,128)(2,1)S(1)} %pad_maximum_fusion.4), channel_id=1, source_target_pairs={{0,8},{2,10},{4,12},{6,14},{8,0},{10,2},{12,4},{14,6},{16,24},{18,... | collective-permute-start | bytes 1572872 | tf_op jit(solution)/shard_map/ppermute | solution.py:1024
  178.3 13.7 %collective-permute-start.26 = (bf16[128,512]{1,0:T(8,128)(2,1)S(1)}, bf16[128,512]{1,0:T(8,128)(2,1)S(1)}, u32[]{:S(2)}, u32[]{:S(2)}) collective-permute-start(bf16[128,512]{1,0:T(8,128)(2,1)S(1)} %add_convert_fusion.22), channel_id=1, source_target_pairs={{0,16},{2,18},{4,20},{6,22},{8,24},{10,26},{12,28},{14,30},{16,0},... | collective-permute-start | bytes 393224 | tf_op jit(solution)/shard_map/ppermute | solution.py:1024
  180.3 13.4 %collective-permute-start.27 = (bf16[128,640]{1,0:T(8,128)(2,1)S(1)}, bf16[128,640]{1,0:T(8,128)(2,1)S(1)}, u32[]{:S(2)}, u32[]{:S(2)}) collective-permute-start(bf16[128,640]{1,0:T(8,128)(2,1)S(1)} %add_convert_fusion.18), channel_id=1, source_target_pairs={{0,16},{2,18},{4,20},{6,22},{8,24},{10,26},{12,28},{14,30},{16,0},... | collective-permute-start | bytes 491528 | tf_op jit(solution)/shard_map/ppermute | solution.py:1024
  183.2 25.2 %collective-permute-start.17 = (bf16[1024,512]{1,0:T(8,128)(2,1)S(1)}, bf16[1024,512]{1,0:T(8,128)(2,1)S(1)}, u32[]{:S(2)}, u32[]{:S(2)}) collective-permute-start(bf16[1024,512]{1,0:T(8,128)(2,1)S(1)} %copy-done.16), channel_id=1, source_target_pairs={{0,1},{1,0},{2,3},{3,2},{4,5},{5,4},{6,7},{7,6},{8,9},{9,8},{10,11... | collective-permute-start | bytes 3145736 | tf_op jit(solution)/shard_map/ppermute | solution.py:1020
  195.2 13.2 %collective-permute-start.29 = (bf16[512,1024]{1,0:T(8,128)(2,1)S(1)}, bf16[512,1024]{1,0:T(8,128)(2,1)S(1)}, u32[]{:S(2)}, u32[]{:S(2)}) collective-permute-start(bf16[512,1024]{1,0:T(8,128)(2,1)S(1)} %pad_maximum_fusion.near_ref), channel_id=1, source_target_pairs={{0,2},{2,0},{4,6},{6,4},{8,10},{10,8},{12,14},{14,12},{16,18},{18,... | collective-permute-start | bytes 3145736 | tf_op jit(solution)/shard_map/ppermute | solution.py:1024
  195.3 13.2 %collective-permute-start.30 = (bf16[512,1024]{1,0:T(8,128)(2,1)S(1)}, bf16[512,1024]{1,0:T(8,128)(2,1)S(1)}, u32[]{:S(2)}, u32[]{:S(2)}) collective-permute-start(bf16[512,1024]{1,0:T(8,128)(2,1)S(1)} %pad_maximum_fusion.1.near_ref), channel_id=1, source_target_pairs={{0,2},{2,0},{4,6},{6,4},{8,10},{10,8},{12,14},{14,12},{16,18},{18,... | collective-permute-start | bytes 3145736 | tf_op jit(solution)/shard_map/ppermute | solution.py:1024
  195.8 11.4 %collective-permute-start.32 = (bf16[128,640]{1,0:T(8,128)(2,1)S(1)}, bf16[128,640]{1,0:T(8,128)(2,1)S(1)}, u32[]{:S(2)}, u32[]{:S(2)}) collective-permute-start(bf16[128,640]{1,0:T(8,128)(2,1)S(1)} %add_convert_fusion.17), channel_id=1, source_target_pairs={{0,4},{2,6},{4,0},{6,2},{8,12},{10,14},{12,8},{14,10},{16,20},{18,... | collective-permute-start | bytes 491528 | tf_op jit(solution)/shard_map/ppermute | solution.py:1024
  (41 other events, 361.1 us)
